TPU v7x, 512 devices: a whole 4x8x8 slice. The times are simulated.
512 devices in a mesh: dp: 64 (over z_hi, y, core), tensor: 8 (over z_lo, x).
Axes of the slice: x: 4, y: 8, z: 8 (z_hi: 4, z_lo: 2; z = z_hi * 2 + z_lo), core: 2. Of those that a mesh axis runs over, the one named last changes fastest.
Arguments:
- tokens: bfloat16 [32768, 8192], P('dp', 'tensor'), may hold values from -6 to 6
- value_weight: bfloat16 [8192, 1024], P('tensor', 'dp'), may hold values from -0.0625 to 0.0625
- adapter_down_weights: bfloat16 [8, 8192, 64], P(None, 'tensor'), may hold values from -0.0625 to 0.0625
- adapter_up_weights: bfloat16 [8, 64, 1024], P(None, None, 'tensor'), may hold values from -0.75 to 0.75
- value_gradient: bfloat16 [32768, 1024], P(('dp', 'tensor')), may hold values from -12 to 12
- block_adapter_index: int32 [256, 1], replicated, may hold values from 0 to 7
- block_live_rows: int32 [256], replicated, may hold values from 1 to 128
Outputs:
- values_out: bfloat16 [32768, 1024], P(('dp', 'tensor'))
- input_gradient: bfloat16 [32768, 8192], P('dp', 'tensor')
- grad_a: float32 [8, 8192, 64], P(None, 'tensor')
- grad_b: float32 [8, 64, 1024], P(None, None, 'tensor')
Inputs may be any that keep to these rules, and one draw needn't show every extreme that they name: `block_adapter_index`: every adapter names at least one block.
All inputs are finite; a program needn't handle non-finite values.
Results may differ from a plain program's by a relative error of at most 0.02.
Values may be sent and summed in bfloat16 or wider, within the bound.
No kernel may reach another device: no remote copies, remote signals or barrier semaphores. Data moves between devices by JAX's collectives and lax.ppermute only.
A program may use at most 64 MiB of HBM per device.

v0:
```python
import jax
import jax.numpy as jnp
from jax import lax
from jax.sharding import PartitionSpec as P

BLK = 128


ADAPTER_SCALE = 2.0


def shards(
    tokens,
    value_weight,
    adapter_down_weights,
    adapter_up_weights,
    value_gradient,
    block_adapter_index,
    block_live_rows,
):
    local_rows = tokens.shape[0]
    tensor_size = lax.axis_size("tensor")
    own_rows = local_rows // tensor_size
    data_index = lax.axis_index("dp")
    tensor_index = lax.axis_index("tensor")
    adapter_count = adapter_down_weights.shape[0]
    local_width = tokens.shape[1]
    rank_columns = adapter_down_weights.shape[2]
    head_columns = adapter_up_weights.shape[2]
    local_blocks = local_rows // BLK
    all_ids = block_adapter_index[:, 0]
    block_indices = lax.dynamic_slice_in_dim(all_ids, data_index * local_blocks, local_blocks)
    block_fill = lax.dynamic_slice_in_dim(block_live_rows, data_index * local_blocks, local_blocks)
    adapter_range = jnp.arange(adapter_count, dtype=jnp.int32)
    block_onehot = (block_indices[:, None] == adapter_range[None, :]).astype(jnp.float32)
    complete_up_weight = lax.all_gather(adapter_up_weights, "tensor", axis=2, tiled=True)
    up_flat = complete_up_weight.reshape(adapter_count * rank_columns, complete_up_weight.shape[2])
    selected_down_weight = adapter_down_weights[block_indices]
    token_block_rows = tokens.reshape(local_blocks, BLK, local_width)
    reduced_part = jnp.einsum(
        "cpe,cev->cpv", token_block_rows, selected_down_weight, preferred_element_type=jnp.float32
    )
    reduced = lax.psum(reduced_part.astype(jnp.bfloat16), "tensor")
    w_full = lax.all_gather(value_weight, "dp", axis=1, tiled=True)
    base_own = lax.psum_scatter(
        jnp.dot(tokens, w_full, preferred_element_type=jnp.float32).astype(jnp.bfloat16),
        "tensor",
        scatter_dimension=0,
        tiled=True,
    ).astype(jnp.float32)
    row_index = tensor_index * own_rows + jnp.arange(own_rows, dtype=jnp.int32)
    row_block = row_index // BLK
    row_ids = block_indices[row_block]
    row_onehot = row_ids[:, None] == adapter_range[None, :]
    reduced_own = lax.dynamic_slice_in_dim(
        reduced.reshape(local_rows, rank_columns), tensor_index * own_rows, own_rows, 0
    )
    spread = (row_onehot[:, :, None].astype(jnp.bfloat16) * reduced_own[:, None, :]).reshape(
        own_rows, adapter_count * rank_columns
    )
    update = jnp.dot(spread, up_flat, preferred_element_type=jnp.float32)
    values_out = (base_own + ADAPTER_SCALE * update).astype(jnp.bfloat16)
    live_rows = row_index % BLK < block_fill[row_block]
    masked = jnp.where(live_rows[:, None], value_gradient, jnp.zeros_like(value_gradient))
    projected = jnp.einsum("kc,mc->km", masked, up_flat, preferred_element_type=jnp.float32)
    grad_low = jnp.sum(
        projected.reshape(own_rows, adapter_count, rank_columns)
        * row_onehot[:, :, None].astype(jnp.float32),
        axis=1,
    ).astype(jnp.bfloat16)
    whole_grad, whole_low = (
        lax.all_gather(masked, "tensor", axis=0, tiled=True),
        lax.all_gather(grad_low, "tensor", axis=0, tiled=True),
    )
    lowrank_block_rows = whole_low.reshape(local_blocks, BLK, rank_columns)
    base_backward = jnp.einsum("kc,dc->kd", whole_grad, w_full, preferred_element_type=jnp.float32)
    adapter_backward = jnp.einsum(
        "sly,say->sla", lowrank_block_rows, selected_down_weight, preferred_element_type=jnp.float32
    ).reshape(local_rows, local_width)
    input_gradient = (base_backward + ADAPTER_SCALE * adapter_backward).astype(jnp.bfloat16)
    down_terms = jnp.einsum(
        "xgj,xgi->xji", token_block_rows, lowrank_block_rows, preferred_element_type=jnp.float32
    )
    down_local = jnp.einsum(
        "ba,bdr->adr", block_onehot, down_terms, precision=lax.Precision.HIGHEST
    )
    grad_cols = lax.dynamic_slice_in_dim(
        whole_grad, tensor_index * head_columns, head_columns, 1
    ).reshape(local_blocks, BLK, head_columns)
    up_terms = jnp.einsum("bkr,bkc->brc", reduced, grad_cols, preferred_element_type=jnp.float32)
    up_local = jnp.einsum("ba,brc->arc", block_onehot, up_terms, precision=lax.Precision.HIGHEST)
    all_onehot = (all_ids[:, None] == adapter_range[None, :]).astype(jnp.float32)
    tallies = jnp.sum(all_onehot * block_live_rows[:, None].astype(jnp.float32), axis=0)
    factor = ADAPTER_SCALE / tallies
    down_sum, up_sum = lax.psum((down_local, up_local), "dp")
    grad_a = down_sum * factor[:, None, None]
    grad_b = up_sum * factor[:, None, None]
    return (values_out, input_gradient, grad_a, grad_b)


def solution(mesh):
    return jax.shard_map(
        shards,
        mesh=mesh,
        in_specs=(
            P("dp", "tensor"),
            P("tensor", "dp"),
            P(None, "tensor", None),
            P(None, None, "tensor"),
            P(("dp", "tensor"), None),
            P(),
            P(),
        ),
        out_specs=(
            P(("dp", "tensor"), None),
            P("dp", "tensor"),
            P(None, "tensor", None),
            P(None, None, "tensor"),
        ),
        check_vma=False,
    )
```

profile of v0, /device:TPU:1, one launch (start us, length us, event | category | flops | bytes accessed | tf_op | source)
XLA Modules:
  0.0 887.0 jit_solution(14993300499443759841)
XLA Ops:
  8.0 0.8 dynamic_slice.17
  9.3 2.6 fusion.21
  11.9 1.6 broadcast_select_fusion
  14.4 1.8 gather_fusion
  16.2 1.1 fusion.5
  18.6 2.6 fusion.23
  21.2 33.2 %all-gather.6.cloned.1.call-done = bf16[8,64,1024]{2,1,0:T(8,128)(2,1)} async-done(((bf16[8,64,128]{2,1,0:T(8,128)(2,1)}), bf16[8,64,1024]{2,1,0:T(8,128)(2,1)}) %all-gather.6.cloned.1.call-update) | async-done | bytes 1048592 | tf_op jit(solution)/shard_map/all_gather | solution.py:36
  54.4 1.9 fusion.4
  56.3 21.8 %all_gather.15 = bf16[512,64]{1,0:T(8,128)(2,1)S(1)} all-gather(bf16[64,64]{1,0:T(8,128)(2,1)S(1)} %fusion.4), channel_id=1, replica_groups=mesh['dp'=64,'tensor'=8] {'tensor'}, dimensions={0}, use_global_device_ids=true | all-gather | bytes 73728 | tf_op jit(solution)/shard_map/all_gather | solution.py:73
  78.1 23.5 %all-gather.8.cloned.1.call-done = bf16[512,1024]{1,0:T(8,128)(2,1)} async-done(((bf16[64,1024]{1,0:T(8,128)(2,1)}), bf16[512,1024]{1,0:T(8,128)(2,1)}) %all-gather.8.cloned.1.call-update) | async-done | bytes 1048592 | tf_op jit(solution)/shard_map/all_gather | solution.py:72
  101.5 0.9 constant_dynamic-slice_fusion
  102.4 85.5 %all-reduce.4.cloned.1.call-done = bf16[4,128,64]{1,2,0:T(8,128)(2,1)} async-done(((bf16[4,128,64]{1,2,0:T(8,128)(2,1)}), bf16[4,128,64]{1,2,0:T(8,128)(2,1)}) %all-reduce.4.cloned.1.call-update) | async-done | bytes 65552 | tf_op jit(solution)/shard_map/psum | solution.py:43
  187.9 1.0 fusion.28
  188.9 1.1 fusion.9
  190.4 3.2 fusion.6
  193.7 87.5 %all-gather.4.cloned.1.call-done = bf16[1024,1024]{0,1:T(8,128)(2,1)} async-done(((bf16[1024,16]{0,1:T(8,128)(2,1)}), bf16[1024,1024]{0,1:T(8,128)(2,1)}) %all-gather.4.cloned.1.call-update) | async-done | bytes 2097168 | tf_op jit(solution)/shard_map/all_gather | solution.py:44
  281.2 3.9 convolution_convert_fusion
  286.3 0.8 copy-done.8
  287.1 2.2 fusion
  289.4 547.3 %all-reduce.6.cloned.1.call-done = (f32[8,1024,64]{1,0,2:T(8,128)}, f32[8,64,128]{2,0,1:T(8,128)}) async-done(((f32[8,1024,64]{1,0,2:T(8,128)}, f32[8,64,128]{2,0,1:T(8,128)}), (f32[8,1024,64]{1,0,2:T(8,128)}, f32[8,64,128]{2,0,1:T(8,128)})) %all-reduce.6.cloned.1.call-update) | async-done | bytes 2359312 | tf_op jit(solution)/shard_map/psum | solution.py:95
  836.7 1.8 broadcast_multiply_fusion
  838.5 2.5 copy.34
  841.9 36.3 %reduce-scatter.2.cloned.1.call-done = bf16[64,1024]{1,0:T(8,128)(2,1)} async-done(((bf16[512,1024]{1,0:T(8,128)(2,1)}), bf16[64,1024]{1,0:T(8,128)(2,1)}) %reduce-scatter.2.cloned.1.call-update) | async-done | bytes 131088 | tf_op jit(solution)/shard_map/reduce_scatter | solution.py:45
  878.2 2.0 fusion.3
  (44 shorter events, 5.8 us)
Async XLA Ops:
  7.2 9.0 %copy-start = (bf16[512,1024]{1,0:T(8,128)(2,1)S(1)}, bf16[512,1024]{1,0:T(8,128)(2,1)}, u32[]{:S(2)}) copy-start(bf16[512,1024]{1,0:T(8,128)(2,1)} %param.7) | copy-start | bytes 3145732
  7.2 47.2 %all-gather.6.cloned.1.call-start = ((), (), s32[]{:S(2)}) async-start(), calls=%async_computation.4 | async-start | bytes 1179648 | tf_op jit(solution)/shard_map/all_gather | solution.py:36
  7.9 93.6 %all-gather.8.cloned.1.call-start = ((), (), s32[]{:S(2)}) async-start(), calls=%async_computation.5 | async-start | bytes 1179648 | tf_op jit(solution)/shard_map/all_gather | solution.py:72
  13.6 40.8 %copy-start.2 = (bf16[64,1024]{1,0:T(8,128)(2,1)S(1)}, bf16[64,1024]{1,0:T(8,128)(2,1)}, u32[]{:S(2)}) copy-start(bf16[64,1024]{1,0:T(8,128)(2,1)} %broadcast_select_fusion) | copy-start | bytes 393220
  13.6 174.3 %all-reduce.4.cloned.1.call-start = ((), (), s32[]{:S(2)}) async-start(), calls=%async_computation.3 | async-start | bytes 131072 | tf_op jit(solution)/shard_map/psum | solution.py:43
  17.3 263.8 %all-gather.4.cloned.1.call-start = ((), (), s32[]{:S(2)}) async-start(), calls=%async_computation.1 | async-start | bytes 2129920 | tf_op jit(solution)/shard_map/all_gather | solution.py:44
  17.9 818.7 %all-reduce.6.cloned.1.call-start = ((), (), s32[]{:S(2)}) async-start(), calls=%async_computation.6 | async-start | bytes 4718592 | tf_op jit(solution)/shard_map/psum | solution.py:95
  193.6 91.4 %copy-start.7 = (s32[256]{0:T(256)S(1)}, s32[256]{0:T(256)}, u32[]{:S(2)}) copy-start(s32[256]{0:T(256)} %param.13) | copy-start | bytes 3076
  193.6 91.4 %copy-start.6 = (s32[256,1]{0,1:T(1,128)S(1)}, s32[256,1]{0,1:T(1,128)}, u32[]{:S(2)}) copy-start(s32[256,1]{0,1:T(1,128)} %param.12) | copy-start | bytes 3076
  193.7 91.6 %copy-start.4 = (bf16[4,128,64]{1,2,0:T(8,128)(2,1)S(1)}, bf16[4,128,64]{1,2,0:T(8,128)(2,1)}, u32[]{:S(2)}) copy-start(bf16[4,128,64]{1,2,0:T(8,128)(2,1)} %all-reduce.4.cloned.1.call-done) | copy-start | bytes 196612
  193.7 684.5 %reduce-scatter.2.cloned.1.call-start = ((), (), s32[]{:S(2)}) async-start(), calls=%async_computation.2 | async-start | bytes 1179648 | tf_op jit(solution)/shard_map/reduce_scatter | solution.py:45
  285.0 1.2 copy-start.5
  285.4 1.7 copy-start.8
  838.5 2.6 copy-start.3
  838.5 39.7 %copy-start.1 = (bf16[8,64,1024]{2,1,0:T(8,128)(2,1)S(1)}, bf16[8,64,1024]{2,1,0:T(8,128)(2,1)}, u32[]{:S(2)}) copy-start(bf16[8,64,1024]{2,1,0:T(8,128)(2,1)} %all-gather.6.cloned.1.call-done) | copy-start | bytes 3145732
Sparse Core Ops, SparseCore 0:
  10.0 44.3 all-gather.5
  57.1 44.4 all-gather.7
  105.0 82.8 all-reduce.3
  191.7 89.4 all-gather.3
  284.9 551.7 all-reduce.5
  839.3 38.7 reduce-scatter.1
where the time goes:
time: 891 us; the launch traced here: 887 us
  waiting for transfers between devices  814 us (91%)
  blocking collectives  21.8 us (2%)
  matrix products  17.1 us (2%)
  between operations  14.3 us (2%)
  other arithmetic  9.62 us (1%)
  local copies, waits for them, and re-layouts  9.44 us (1%)
    psum x1, waiting for transfers between devices, shards(): down_sum, up_sum = lax.psum((down_local, up_local), 'dp')  547 us
    all_gather x1, waiting for transfers between devices, shards(): w_full = lax.all_gather(value_weight, 'dp', axis=1, tiled=True)  87.5 us
    psum x1, waiting for transfers between devices, shards(): reduced = lax.psum(reduced_part.astype(jnp.bfloat16), 'tensor')  85.5 us
    reduce_scatter x1, waiting for transfers between devices, shards(): lax.psum_scatter(jnp.dot(tokens, w_full, preferred_element_type=jnp.float...  36.3 us
    all_gather x1, waiting for transfers between devices, shards(): lax.all_gather(adapter_up_weights, 'tensor', axis=2, tiled=True)  33.2 us
    all_gather x1, waiting for transfers between devices, shards(): lax.all_gather(masked, 'tensor', axis=0, tiled=True)  23.5 us
    all_gather x1, blocking collectives, shards(): lax.all_gather(grad_low, 'tensor', axis=0, tiled=True)  21.8 us
  transfers between devices with their start and end apart: 6, of which 6 were waited for; matrix products, arithmetic and copies ran while one was open for 4% of the time, Pallas kernels for 0%

commit v1 on v0

v1 whole, which is shorter than its diff:
```python
import jax
import jax.numpy as jnp
from jax import lax
from jax.experimental import pallas as pl
from jax.experimental.pallas import tpu as pltpu
from jax.sharding import PartitionSpec as P

BLK = 128
ADAPTER_SCALE = 2.0
F32 = jnp.float32
BF16 = jnp.bfloat16

TENSOR = 8
PEERS = 32
ROWS = 512
OWN = 64
BLOCKS = 4
WIDTH = 1024
COLS = 1024
HEAD = 128
RANK = 64
ADAPTERS = 8
TERM = WIDTH + HEAD
SEND_UP = 512
SEND_RED = 768
SEND = 1024

SMEM = pl.BlockSpec(memory_space=pltpu.SMEM)
VMEM = pl.BlockSpec(memory_space=pltpu.VMEM)
NT = (((1,), (1,)), ((), ()))
TN = (((0,), (0,)), ((), ()))


def call(kernel, ins, outs, flops, scratch=(), vmem=32):
    moved = sum(x.size * x.dtype.itemsize for x in (*ins, *outs))
    many = len(outs) > 1
    return pl.pallas_call(
        kernel,
        out_shape=tuple(outs) if many else outs[0],
        in_specs=[SMEM if x.dtype == jnp.int32 and x.ndim == 1 else VMEM for x in ins],
        out_specs=(VMEM,) * len(outs) if many else VMEM,
        scratch_shapes=list(scratch),
        compiler_params=pltpu.CompilerParams(vmem_limit_bytes=vmem * 1024 * 1024),
        cost_estimate=pl.CostEstimate(flops=flops, bytes_accessed=moved, transcendentals=0),
    )(*ins)


def out(shape, dtype=BF16):
    return jax.ShapeDtypeStruct(shape, dtype)


def dot(a, b, dims=(((1,), (0,)), ((), ()))):
    return lax.dot_general(a, b, dims, preferred_element_type=F32)


def pack_kernel(idx, live, pos, grad, up, tokens, down, send):
    data, tensor = pos[0], pos[1]
    block = tensor // 2
    row = (tensor % 2) * OWN + lax.broadcasted_iota(jnp.int32, (OWN, 128), 0)
    keep = row < live[data * BLOCKS + block]
    for k in range(COLS // 128):
        part = grad[:, k * 128 : (k + 1) * 128]
        part = jnp.where(keep, part.astype(F32), 0.0).astype(BF16)
        for p in range(TENSOR):
            send[p, k * OWN : (k + 1) * OWN, :] = part
    for b in range(BLOCKS):
        a = idx[data * BLOCKS + b]
        rows = up[a]
        red = dot(down[a], tokens[b * BLK : (b + 1) * BLK, :], NT).astype(BF16)
        for p in range(TENSOR):
            send[p, SEND_UP + b * RANK : SEND_UP + (b + 1) * RANK, :] = rows
            send[p, SEND_RED + b * RANK : SEND_RED + (b + 1) * RANK, :] = red


def terms_kernel(pos, got, tokens, masked, low, mine, theirs, update, red, ups, terms, block_update):
    data, tensor = pos[0], pos[1]
    core = data % 2
    for p in range(TENSOR):
        for k in range(COLS // 128):
            masked[p * OWN : (p + 1) * OWN, k * 128 : (k + 1) * 128] = got[p, k * OWN : (k + 1) * OWN, :]
        ups[:, p * HEAD : (p + 1) * HEAD] = got[p, SEND_UP:SEND_RED, :]
    total = got[0, SEND_RED:SEND, :].astype(F32)
    for p in range(1, TENSOR):
        total += got[p, SEND_RED:SEND, :].astype(F32)
    red[...] = total.astype(BF16)
    column = pl.multiple_of(tensor * OWN, OWN)
    for b in range(BLOCKS):
        rank = slice(b * RANK, (b + 1) * RANK)
        rows = slice(b * BLK, (b + 1) * BLK)
        projected = dot(ups[rank, :], masked[rows, :], NT).astype(BF16)
        low[rank, :] = projected
        terms[rank, :WIDTH] = dot(projected, tokens[rows, :]).astype(BF16)
        own = jnp.concatenate([got[2 * b, pl.ds(column, OWN), :], got[2 * b + 1, pl.ds(column, OWN), :]], axis=0)
        terms[rank, WIDTH:] = dot(red[rank, :], own).astype(BF16)
    for b in range(BLOCKS):
        here = pl.multiple_of(b * RANK + core * 32, 32)
        there = pl.multiple_of(b * RANK + (1 - core) * 32, 32)
        mine[b * 32 : (b + 1) * 32, :] = terms[pl.ds(here, 32), :]
        theirs[b * 32 : (b + 1) * 32, :] = terms[pl.ds(there, 32), :]
    first = pl.multiple_of((tensor // 2) * RANK, RANK)
    block_update[...] = ADAPTER_SCALE * dot(red[pl.ds(first, RANK), :], ups[pl.ds(first, RANK), :], TN)
    update[...] = block_update[pl.ds(pl.multiple_of((tensor % 2) * OWN, OWN), OWN), :]


def scatter_kernel(idx, pos, mine, theirs, by_peer):
    data = pos[0]
    row = lax.broadcasted_iota(jnp.int32, (PEERS * ADAPTERS, 128), 0)
    column = lax.broadcasted_iota(jnp.int32, (PEERS * ADAPTERS, 128), 1)

    def chosen(owner):
        block = column // 32
        adapter = jnp.where(
            block < 2,
            jnp.where(block == 0, idx[owner * BLOCKS], idx[owner * BLOCKS + 1]),
            jnp.where(block == 2, idx[owner * BLOCKS + 2], idx[owner * BLOCKS + 3]),
        )
        hit = (column % 32 == row // ADAPTERS) & (adapter == row % ADAPTERS)
        return jnp.where(hit, 1.0, 0.0).astype(BF16)

    sibling = data + 1 - 2 * (data % 2)
    by_peer[...] = (dot(chosen(data), mine[...]) + dot(chosen(sibling), theirs[...])).astype(BF16)


def total_kernel(idx, live, parts, spread):
    total = parts[0:16, :].astype(F32)
    for p in range(1, PEERS // 2):
        total += parts[p * 16 : (p + 1) * 16, :].astype(F32)
    total = total[:8, :] + total[8:, :]
    row = lax.broadcasted_iota(jnp.int32, (ADAPTERS, 128), 0)
    factor = jnp.zeros((ADAPTERS, 128), F32)
    for e in range(ADAPTERS):
        count = jnp.sum(jnp.where(idx[...] == e, live[...], 0).astype(F32), keepdims=True)
        factor = jnp.where(row == e, ADAPTER_SCALE / jnp.broadcast_to(count, (ADAPTERS, 128)), factor)
    for k in range(TERM // 128):
        lanes = slice(k * 128, (k + 1) * 128)
        scaled = total[:, lanes] * factor
        both = jnp.concatenate([scaled, scaled], axis=0).astype(BF16)
        for p in range(PEERS // 2):
            spread[p * 16 : (p + 1) * 16, lanes] = both


def unpack_kernel(pos, mine, theirs, grad_a, grad_b):
    core = pos[0] % 2
    row = lax.broadcasted_iota(jnp.int32, (256, 256), 0)
    column = lax.broadcasted_iota(jnp.int32, (256, 256), 1)
    order = jnp.where(column == (row % PEERS) * ADAPTERS + row // PEERS, 1.0, 0.0).astype(BF16)
    for half, rows in ((core, mine), (1 - core, theirs)):
        first = pl.multiple_of(half * PEERS, PEERS)
        for k in range(TERM // 128):
            lanes = slice(k * 128, (k + 1) * 128)
            part = dot(order, rows[:, lanes])
            for e in range(ADAPTERS):
                piece = part[e * PEERS : (e + 1) * PEERS, :]
                if k < WIDTH // 128:
                    grad_a[e, pl.ds(first, PEERS), lanes] = piece
                else:
                    grad_b[e, pl.ds(first, PEERS), :] = piece


def base_kernel(tokens, weight, base):
    for b in range(BLOCKS):
        rows = slice(b * BLK, (b + 1) * BLK)
        base[rows, :] = dot(tokens[rows, :], weight[...], NT).astype(BF16)


def input_kernel(idx, pos, masked, weight, low, down, grad):
    data = pos[0]
    for b in range(BLOCKS):
        rows = slice(b * BLK, (b + 1) * BLK)
        adapter = dot(low[b * RANK : (b + 1) * RANK, :], down[idx[data * BLOCKS + b]], TN)
        grad[rows, :] = (dot(masked[rows, :], weight[...]) + ADAPTER_SCALE * adapter).astype(BF16)


def shards(tokens, value_weight, down, up, value_gradient, block_adapter_index, block_live_rows):
    same_core = [list(range(core, 2 * PEERS, 2)) for core in range(2)]
    sibling = [(i, i ^ 1) for i in range(2 * PEERS)]
    pos = jnp.stack([lax.axis_index("dp"), lax.axis_index("tensor")]).astype(jnp.int32)
    idx = block_adapter_index[:, 0]
    live = block_live_rows
    down_t = jnp.swapaxes(down, 1, 2)
    weight = jnp.swapaxes(lax.all_gather(value_weight, "dp", axis=1, tiled=True), 0, 1)

    send = call(
        pack_kernel, (idx, live, pos, value_gradient, up, tokens, down_t),
        (out((TENSOR, SEND, 128)),), 2 * ROWS * WIDTH * RANK,
    )
    got = lax.all_to_all(send, "tensor", 0, 0, tiled=True)
    masked, low, mine, theirs, update = call(
        terms_kernel, (pos, got, tokens),
        (out((ROWS, COLS)), out((BLOCKS * RANK, BLK)), out((128, TERM)), out((128, TERM)), out((OWN, COLS), F32)),
        6 * ROWS * WIDTH * RANK,
        (
            pltpu.VMEM((BLOCKS * RANK, BLK), BF16),
            pltpu.VMEM((BLOCKS * RANK, COLS), BF16),
            pltpu.VMEM((BLOCKS * RANK, TERM), BF16),
            pltpu.VMEM((BLK, COLS), F32),
        ),
    )
    theirs = lax.ppermute(theirs, "dp", sibling)
    by_peer = call(scatter_kernel, (idx, pos, mine, theirs), (out((PEERS * ADAPTERS, TERM)),), 2 * 256 * 256 * TERM)
    parts = lax.all_to_all(by_peer, "dp", 0, 0, tiled=True, axis_index_groups=same_core)
    spread = call(
        total_kernel, (idx.reshape(2, 128), live.reshape(2, 128), parts),
        (out((PEERS * ADAPTERS, TERM)),), 256 * TERM,
    )
    half = lax.all_to_all(spread, "dp", 0, 0, tiled=True, axis_index_groups=same_core)
    other = lax.ppermute(half, "dp", sibling)
    grad_a, grad_b = call(
        unpack_kernel, (pos, half, other),
        (out((ADAPTERS, RANK, WIDTH), F32), out((ADAPTERS, RANK, HEAD), F32)), 4 * 256 * 256 * TERM,
    )

    base = call(base_kernel, (tokens, weight), (out((ROWS, COLS)),), 2 * ROWS * WIDTH * COLS)
    base_parts = lax.all_to_all(base, "tensor", 0, 0, tiled=True).reshape(TENSOR, OWN, COLS)
    input_gradient = call(
        input_kernel, (idx, pos, masked, weight, low, down_t), (out((ROWS, WIDTH)),),
        2 * ROWS * WIDTH * (COLS + RANK),
    )
    values_out = (jnp.sum(base_parts.astype(F32), axis=0) + update).astype(BF16)
    return values_out, input_gradient, jnp.swapaxes(grad_a, 1, 2), grad_b


def solution(mesh):
    return jax.shard_map(
        shards,
        mesh=mesh,
        in_specs=(
            P("dp", "tensor"),
            P("tensor", "dp"),
            P(None, "tensor", None),
            P(None, None, "tensor"),
            P(("dp", "tensor"), None),
            P(),
            P(),
        ),
        out_specs=(
            P(("dp", "tensor"), None),
            P("dp", "tensor"),
            P(None, "tensor", None),
            P(None, None, "tensor"),
        ),
        check_vma=False,
    )
```

time: 891 us -> 158 us (0.18)
  waiting for transfers between devices: 814 us -> 54.6 us
  starting transfers between devices: 0.24 us -> 27.2 us
  matrix products: 17.1 us -> 0 us
  Pallas kernels: 0 us -> 15.6 us
  blocking collectives: 21.8 us -> 32.5 us
    psum x2 -> x0, waiting for transfers between devices: 633 us -> none  [the longest x1 547 us: shards(): down_sum, up_sum = lax.psum((down_local, up_local), 'dp')]
    all_gather x3 -> x1, waiting for transfers between devices: 144 us -> 20 us  [shards(): lax.all_gather(value_weight, 'dp', axis=1, tiled=True)]
    reduce_scatter x1 -> x0, waiting for transfers between devices: 36.3 us -> none  [shards(): lax.psum_scatter(jnp.dot(tokens, w_full, preferred_element_type=jnp.float...]
    all_to_all x0 -> x3, waiting for transfers between devices: none -> 32.7 us  [the longest x1 24.4 us: shards(): got = lax.all_to_all(send, 'tensor', 0, 0, tiled=True)]
    all_to_all x0 -> x1, blocking collectives: none -> 32.5 us  [shards(): lax.all_to_all(by_peer, 'dp', 0, 0, tiled=True, axis_index_groups=same_core)]
    all_gather x1 -> x0, blocking collectives: 21.8 us -> none  [shards(): lax.all_gather(grad_low, 'tensor', axis=0, tiled=True)]
    all_to_all x0 -> x3, starting transfers between devices: none -> 21 us  [the longest x1 8.19 us: shards(): lax.all_to_all(spread, 'dp', 0, 0, tiled=True, axis_index_groups=same_core)]
    dot_general x10 -> x0, matrix products: 17.1 us -> none  [the longest x1 3.86 us: shards(): jnp.dot(tokens, w_full, preferred_element_type=jnp.float32)]
  transfers between devices with their start and end apart: 6 -> 6, of which waited for: 6 -> 4; matrix products, arithmetic and copies ran while one was open for 4% -> 1% of each run, Pallas kernels for 0% -> 7%
where the time goes in v1:
time: 158 us; the launch traced here: 157 us
  waiting for transfers between devices  54.6 us (35%)
  blocking collectives  32.5 us (21%)
  starting transfers between devices  27.2 us (17%)
  Pallas kernels  15.6 us (10%)
  between operations  14.1 us (9%)
  local copies, waits for them, and re-layouts  10.7 us (7%)
  other arithmetic  2.18 us (1%)
    all_to_all x1, blocking collectives, shards(): lax.all_to_all(by_peer, 'dp', 0, 0, tiled=True, axis_index_groups=same_core)  32.5 us
    all_to_all x1, waiting for transfers between devices, shards(): got = lax.all_to_all(send, 'tensor', 0, 0, tiled=True)  24.4 us
    all_gather x1, waiting for transfers between devices, shards(): lax.all_gather(value_weight, 'dp', axis=1, tiled=True)  20 us
    pallas_call x7, Pallas kernels, call(): pl.pallas_call(kernel, out_shape=tuple(outs) if many else outs[0], in_spe...  15.6 us
    unnamed x30, local copies, waits for them, and re-layouts  10.7 us
    all_to_all x1, waiting for transfers between devices, shards(): lax.all_to_all(base, 'tensor', 0, 0, tiled=True).reshape(TENSOR, OWN, COLS)  8.28 us
    all_to_all x1, starting transfers between devices, shards(): lax.all_to_all(spread, 'dp', 0, 0, tiled=True, axis_index_groups=same_core)  8.19 us
    all_to_all x1, starting transfers between devices, shards(): got = lax.all_to_all(send, 'tensor', 0, 0, tiled=True)  6.79 us
  transfers between devices with their start and end apart: 6, of which 4 were waited for; matrix products, arithmetic and copies ran while one was open for 1% of the time, Pallas kernels for 7%

profile of v1, /device:TPU:1, one launch (start us, length us, event | category | flops | bytes accessed | tf_op | source)
XLA Modules:
  0.0 157.1 jit_solution(9008096855200797928)
XLA Ops:
  7.2 1.2 copy-done
  8.5 1.2 copy-done.5
  12.9 1.1 shard_map.103
  14.0 1.3 copy-done.4
  15.3 6.8 %all-to-all-start.1 = ((bf16[8,1024,128]{2,1,0:T(8,128)(2,1)}), bf16[8,1024,128]{2,1,0:T(8,128)(2,1)S(1)}, u32[]{:S(2)}, u32[]{:S(2)}) async-start(bf16[8,1024,128]{2,1,0:T(8,128)(2,1)} %copy-done.4), calls=%async_computation.1 | async-start | bytes 4194304 | tf_op jit(solution)/shard_map/all_to_all | solution.py:187
  22.8 24.4 %all-to-all-done.1.got = bf16[8,1024,128]{2,1,0:T(8,128)(2,1)S(1)} async-done(((bf16[8,1024,128]{2,1,0:T(8,128)(2,1)}), bf16[8,1024,128]{2,1,0:T(8,128)(2,1)S(1)}, u32[]{:S(2)}, u32[]{:S(2)}) %all-to-all-start.1) | async-done | bytes 2097184 | tf_op jit(solution)/shard_map/all_to_all | solution.py:187
  47.3 2.2 %shard_map.104 = (bf16[512,1024]{1,0:T(8,128)(2,1)S(1)}, bf16[256,128]{1,0:T(8,128)(2,1)S(1)}, bf16[128,1152]{1,0:T(8,128)(2,1)S(1)}, bf16[128,1152]{1,0:T(8,128)(2,1)S(1)}, f32[64,1024]{1,0:T(8,128)S(1)}) custom-call(s32[2]{0:T(128)S(1)} %pad_add_fusion.pos, bf16[8,1024,128]{2,1,0:T(8,128)(2,1)S(1)} %all-to-all-done.1.got, bf16[512,1024]{1,0:T(8,128)(2,1)S(1)} %copy-done.1), custom_call_target="tpu_custom_call" | custom-call | flops 201326592 | bytes 5111816 | tf_op jit(solution)/shard_map/pallas_call | solution.py:37
  49.5 1.0 copy-done.7
  50.4 3.7 %collective-permute-start = (bf16[128,1152]{1,0:T(8,128)(2,1)S(1)}, bf16[128,1152]{1,0:T(8,128)(2,1)S(1)}, u32[]{:S(2)}, u32[]{:S(2)}) collective-permute-start(bf16[128,1152]{1,0:T(8,128)(2,1)S(1)} %get-tuple-element.15), channel_id=1, source_target_pairs={{0,8},{8,0},{16,24},{24,16},{32,40},{40,32},{48,56},{56,48},{64,72... | collective-permute-start | bytes 884744 | tf_op jit(solution)/shard_map/ppermute | solution.py:199
  54.2 1.2 collective-permute-done.theirs
  55.3 1.0 shard_map.106
  56.4 32.5 %all_to_all.36 = bf16[32,8,1152]{2,1,0:T(8,128)(2,1)S(1)} all-to-all(bf16[32,8,1152]{2,1,0:T(8,128)(2,1)S(1)} %bitcast.17), channel_id=1, replica_groups={{0,16,32,48,64,80,96,112,128,144,160,176,192,208,224,240,256,272,288,30..., dimensions={0} | all-to-all | bytes 1179648 | tf_op jit(solution)/shard_map/all_to_all | solution.py:201
  88.9 1.1 shard_map.107
  89.9 8.2 %all-to-all-start.3 = ((bf16[32,8,1152]{2,1,0:T(8,128)(2,1)}), bf16[32,8,1152]{2,1,0:T(8,128)(2,1)}, u32[]{:S(2)}, u32[]{:S(2)}) async-start(bf16[32,8,1152]{2,1,0:T(8,128)(2,1)} %bitcast.10), calls=%async_computation.3 | async-start | bytes 1179648 | tf_op jit(solution)/shard_map/all_to_all | solution.py:206
  98.1 20.0 %all-gather.2.cloned.1.call-done = bf16[1024,1024]{0,1:T(8,128)(2,1)} async-done(((bf16[1024,16]{0,1:T(8,128)(2,1)}), bf16[1024,1024]{0,1:T(8,128)(2,1)}) %all-gather.2.cloned.1.call-update) | async-done | bytes 2097168 | tf_op jit(solution)/shard_map/all_gather | solution.py:181
  118.2 1.6 %copy-done.2 = bf16[1024,1024]{0,1:T(8,128)(2,1)S(1)} copy-done((bf16[1024,1024]{0,1:T(8,128)(2,1)S(1)}, bf16[1024,1024]{0,1:T(8,128)(2,1)}, u32[]{:S(2)}) %copy-start.2) | copy-done | bytes 2097176
  119.8 3.8 %shard_map.102 = bf16[512,1024]{1,0:T(8,128)(2,1)} custom-call(bf16[512,1024]{1,0:T(8,128)(2,1)S(1)} %copy-done.1, bf16[1024,1024]{1,0:T(8,128)(2,1)S(1)} %bitcast.13), custom_call_target="tpu_custom_call" | custom-call | flops 1073741824 | bytes 4194304 | tf_op jit(solution)/shard_map/pallas_call | solution.py:37
  123.6 6.1 %all-to-all-start = ((bf16[8,64,1024]{2,1,0:T(8,128)(2,1)}), bf16[8,64,1024]{2,1,0:T(8,128)(2,1)}, u32[]{:S(2)}, u32[]{:S(2)}) async-start(bf16[8,64,1024]{2,1,0:T(8,128)(2,1)} %bitcast.1), calls=%async_computation | async-start | bytes 2097152 | tf_op jit(solution)/shard_map/all_to_all | solution.py:214
  129.7 2.5 %collective-permute-start.1 = (bf16[256,1152]{1,0:T(8,128)(2,1)}, bf16[256,1152]{1,0:T(8,128)(2,1)}, u32[]{:S(2)}, u32[]{:S(2)}) collective-permute-start(bf16[256,1152]{1,0:T(8,128)(2,1)} %bitcast.11.mine), channel_id=1, source_target_pairs={{0,8},{8,0},{16,24},{24,16},{32,40},{40,32},{48,56},{56,48},{64,72... | collective-permute-start | bytes 1769480 | tf_op jit(solution)/shard_map/ppermute | solution.py:207
  132.2 1.2 copy-done.8
  133.4 3.1 %shard_map.105 = bf16[512,1024]{1,0:T(8,128)(2,1)} custom-call(s32[256]{0:T(256)S(1)} %bitcast.22, s32[2]{0:T(128)S(1)} %pad_add_fusion.pos, bf16[512,1024]{1,0:T(8,128)(2,1)S(1)} %copy-done.8, bf16[1024,1024]{1,0:T(8,128)(2,1)S(1)} %bitcast.14, bf16[256,128]{1,0:T(8,128)(2,1)S(1)} %get-tuple-element.13.low, bf16[8,64,1024]{2,1,0:T(8,128)(2,1)S(1)} %bitcast.16), custom_call_target="tpu_custom_call" | custom-call | flops 1140850688 | bytes 5309448 | tf_op jit(solution)/shard_map/pallas_call | solution.py:37
  136.5 8.3 %all-to-all-done = bf16[8,64,1024]{2,1,0:T(8,128)(2,1)} async-done(((bf16[8,64,1024]{2,1,0:T(8,128)(2,1)}), bf16[8,64,1024]{2,1,0:T(8,128)(2,1)}, u32[]{:S(2)}, u32[]{:S(2)}) %all-to-all-start) | async-done | bytes 1048608 | tf_op jit(solution)/shard_map/all_to_all | solution.py:214
  144.7 1.4 convert_reduce_fusion
  146.9 3.4 %shard_map.108 = (f32[8,64,1024]{2,1,0:T(8,128)}, f32[8,64,128]{2,1,0:T(8,128)}) custom-call(s32[2]{0:T(128)S(1)} %pad_add_fusion.pos, bf16[256,1152]{1,0:T(8,128)(2,1)} %bitcast.11.mine, bf16[256,1152]{1,0:T(8,128)(2,1)} %collective-permute-done.1.theirs), custom_call_target="tpu_custom_call" | custom-call | flops 301989888 | bytes 3538952 | tf_op jit(solution)/shard_map/pallas_call | solution.py:37
  (30 shorter events, 4.7 us)
Async XLA Ops:
  7.2 1.2 copy-start
  8.5 1.2 copy-start.5
  9.7 0.9 copy-start.9
  10.6 0.9 copy-start.10
  11.5 0.7 copy-start.11
  12.2 0.7 copy-start.13
  14.0 1.3 copy-start.4
  15.3 32.0 %copy-start.1 = (bf16[512,1024]{1,0:T(8,128)(2,1)S(1)}, bf16[512,1024]{1,0:T(8,128)(2,1)}, u32[]{:S(2)}) copy-start(bf16[512,1024]{1,0:T(8,128)(2,1)} %tokens.5) | copy-start | bytes 3145732
  15.3 32.0 %all-to-all-start.1 = ((bf16[8,1024,128]{2,1,0:T(8,128)(2,1)}), bf16[8,1024,128]{2,1,0:T(8,128)(2,1)S(1)}, u32[]{:S(2)}, u32[]{:S(2)}) async-start(bf16[8,1024,128]{2,1,0:T(8,128)(2,1)} %copy-done.4), calls=%async_computation.1 | async-start | bytes 4194304 | tf_op jit(solution)/shard_map/all_to_all | solution.py:187
  22.1 33.3 %copy-start.12 = (s32[256,1]{0,1:T(1,128)S(1)}, s32[256,1]{0,1:T(1,128)}, u32[]{:S(2)}) copy-start(s32[256,1]{0,1:T(1,128)} %param.12) | copy-start | bytes 3076
  22.1 96.1 %all-gather.2.cloned.1.call-start = ((), (), s32[]{:S(2)}) async-start(), calls=%async_computation.4 | async-start | bytes 2129920 | tf_op jit(solution)/shard_map/all_gather | solution.py:181
  22.8 66.1 %copy-start.14 = (s32[256]{0:T(256)S(1)}, s32[256]{0:T(256)}, u32[]{:S(2)}) copy-start(s32[256]{0:T(256)} %live.1) | copy-start | bytes 3076
  49.5 1.0 copy-start.7
  50.4 4.9 %collective-permute-start = (bf16[128,1152]{1,0:T(8,128)(2,1)S(1)}, bf16[128,1152]{1,0:T(8,128)(2,1)S(1)}, u32[]{:S(2)}, u32[]{:S(2)}) collective-permute-start(bf16[128,1152]{1,0:T(8,128)(2,1)S(1)} %get-tuple-element.15), channel_id=1, source_target_pairs={{0,8},{8,0},{16,24},{24,16},{32,40},{40,32},{48,56},{56,48},{64,72... | collective-permute-start | bytes 884744 | tf_op jit(solution)/shard_map/ppermute | solution.py:199
  89.9 33.7 %all-to-all-start.3 = ((bf16[32,8,1152]{2,1,0:T(8,128)(2,1)}), bf16[32,8,1152]{2,1,0:T(8,128)(2,1)}, u32[]{:S(2)}, u32[]{:S(2)}) async-start(bf16[32,8,1152]{2,1,0:T(8,128)(2,1)} %bitcast.10), calls=%async_computation.3 | async-start | bytes 1179648 | tf_op jit(solution)/shard_map/all_to_all | solution.py:206
  118.2 1.6 %copy-start.2 = (bf16[1024,1024]{0,1:T(8,128)(2,1)S(1)}, bf16[1024,1024]{0,1:T(8,128)(2,1)}, u32[]{:S(2)}) copy-start(bf16[1024,1024]{0,1:T(8,128)(2,1)} %all-gather.2.cloned.1.call-done) | copy-start | bytes 6291460
  119.8 12.4 %copy-start.6 = (bf16[8,1024,64]{1,2,0:T(8,128)(2,1)S(1)}, bf16[8,1024,64]{1,2,0:T(8,128)(2,1)}, u32[]{:S(2)}) copy-start(bf16[8,1024,64]{1,2,0:T(8,128)(2,1)} %param.9) | copy-start | bytes 3145732
  123.6 8.6 %copy-start.3 = (bf16[1024,1024]{0,1:T(8,128)(2,1)S(1)}, bf16[1024,1024]{0,1:T(8,128)(2,1)}, u32[]{:S(2)}) copy-start(bf16[1024,1024]{0,1:T(8,128)(2,1)} %all-gather.2.cloned.1.call-done) | copy-start | bytes 6291460
  123.6 21.1 %all-to-all-start = ((bf16[8,64,1024]{2,1,0:T(8,128)(2,1)}), bf16[8,64,1024]{2,1,0:T(8,128)(2,1)}, u32[]{:S(2)}, u32[]{:S(2)}) async-start(bf16[8,64,1024]{2,1,0:T(8,128)(2,1)} %bitcast.1), calls=%async_computation | async-start | bytes 2097152 | tf_op jit(solution)/shard_map/all_to_all | solution.py:214
  129.7 17.2 %collective-permute-start.1 = (bf16[256,1152]{1,0:T(8,128)(2,1)}, bf16[256,1152]{1,0:T(8,128)(2,1)}, u32[]{:S(2)}, u32[]{:S(2)}) collective-permute-start(bf16[256,1152]{1,0:T(8,128)(2,1)} %bitcast.11.mine), channel_id=1, source_target_pairs={{0,8},{8,0},{16,24},{24,16},{32,40},{40,32},{48,56},{56,48},{64,72... | collective-permute-start | bytes 1769480 | tf_op jit(solution)/shard_map/ppermute | solution.py:207
  132.2 1.2 copy-start.8
Sparse Core Ops, SparseCore 0:
  26.3 91.8 all-gather.1

commit v2 on v1

--- a/solution.py
+++ b/solution.py
@@ -3,6 +3,7 @@
 from jax import lax
 from jax.experimental import pallas as pl
 from jax.experimental.pallas import tpu as pltpu
+from jax.sharding import Mesh
 from jax.sharding import PartitionSpec as P
 
 BLK = 128
@@ -21,23 +22,34 @@
 RANK = 64
 ADAPTERS = 8
 TERM = WIDTH + HEAD
+Z_HI = 4
+STRIPE = 16
+PLANE = COLS // Z_HI
+AXES = {"z_hi": Z_HI, "y": 8, "core": 2, "z_lo": 2, "x": 4}
+DP = ("z_hi", "y", "core")
+PEER = ("z_hi", "y")
+TP = ("z_lo", "x")
 SEND_UP = 512
 SEND_RED = 768
 SEND = 1024
 
 SMEM = pl.BlockSpec(memory_space=pltpu.SMEM)
+ANY = pl.BlockSpec(memory_space=pl.ANY)
 VMEM = pl.BlockSpec(memory_space=pltpu.VMEM)
 NT = (((1,), (1,)), ((), ()))
 TN = (((0,), (0,)), ((), ()))
 
 
-def call(kernel, ins, outs, flops, scratch=(), vmem=32):
+def call(kernel, ins, outs, flops, scratch=(), vmem=32, in_place=()):
     moved = sum(x.size * x.dtype.itemsize for x in (*ins, *outs))
     many = len(outs) > 1
     return pl.pallas_call(
         kernel,
         out_shape=tuple(outs) if many else outs[0],
-        in_specs=[SMEM if x.dtype == jnp.int32 and x.ndim == 1 else VMEM for x in ins],
+        in_specs=[
+            SMEM if x.dtype == jnp.int32 and x.ndim == 1 else ANY if i in in_place else VMEM
+            for i, x in enumerate(ins)
+        ],
         out_specs=(VMEM,) * len(outs) if many else VMEM,
         scratch_shapes=list(scratch),
         compiler_params=pltpu.CompilerParams(vmem_limit_bytes=vmem * 1024 * 1024),
@@ -53,32 +65,66 @@
     return lax.dot_general(a, b, dims, preferred_element_type=F32)
 
 
-def pack_kernel(idx, live, pos, grad, up, tokens, down, send):
+def after(value, earlier):
+    return pl.pallas_call(
+        lambda value_in, earlier_in, value_out: None,
+        out_shape=out(value.shape, value.dtype),
+        in_specs=[ANY, ANY],
+        out_specs=ANY,
+        input_output_aliases={0: 0},
+        cost_estimate=pl.CostEstimate(flops=0, bytes_accessed=0, transcendentals=0),
+    )(value, earlier)
+
+
+def pack_kernel(idx, live, pos, grad_in, up_in, tokens_in, down_in, send, grad, up, tokens, down, sems):
     data, tensor = pos[0], pos[1]
+    copies = []
+    for b in range(BLOCKS):
+        a = idx[data * BLOCKS + b]
+        rows = pl.ds(b * BLK, BLK)
+        copies.append(
+            (
+                pltpu.make_async_copy(down_in.at[a], down.at[b], sems.at[b]),
+                pltpu.make_async_copy(tokens_in.at[rows], tokens.at[rows], sems.at[BLOCKS + b]),
+                pltpu.make_async_copy(up_in.at[a], up.at[b], sems.at[2 * BLOCKS + b]),
+            )
+        )
+    grad_copy = pltpu.make_async_copy(grad_in, grad, sems.at[3 * BLOCKS])
+    grad_copy.start()
+    for group in copies:
+        for copy in group:
+            copy.start()
     block = tensor // 2
     row = (tensor % 2) * OWN + lax.broadcasted_iota(jnp.int32, (OWN, 128), 0)
     keep = row < live[data * BLOCKS + block]
+    grad_copy.wait()
     for k in range(COLS // 128):
         part = grad[:, k * 128 : (k + 1) * 128]
         part = jnp.where(keep, part.astype(F32), 0.0).astype(BF16)
         for p in range(TENSOR):
             send[p, k * OWN : (k + 1) * OWN, :] = part
     for b in range(BLOCKS):
-        a = idx[data * BLOCKS + b]
-        rows = up[a]
-        red = dot(down[a], tokens[b * BLK : (b + 1) * BLK, :], NT).astype(BF16)
+        for copy in copies[b]:
+            copy.wait()
+        rows = up[b]
+        red = dot(down[b], tokens[b * BLK : (b + 1) * BLK, :], NT).astype(BF16)
         for p in range(TENSOR):
             send[p, SEND_UP + b * RANK : SEND_UP + (b + 1) * RANK, :] = rows
             send[p, SEND_RED + b * RANK : SEND_RED + (b + 1) * RANK, :] = red
 
 
-def terms_kernel(pos, got, tokens, masked, low, mine, theirs, update, red, ups, terms, block_update):
+def unpack_rows(got, masked):
+    for p in range(TENSOR):
+        for k in range(COLS // 128):
+            masked[p * OWN : (p + 1) * OWN, k * 128 : (k + 1) * 128] = got[p, k * OWN : (k + 1) * OWN, :]
+
+
+def terms_kernel(pos, got, tokens, low, mine, theirs, update, masked, red, ups, terms, block_update):
     data, tensor = pos[0], pos[1]
     core = data % 2
     for p in range(TENSOR):
-        for k in range(COLS // 128):
-            masked[p * OWN : (p + 1) * OWN, k * 128 : (k + 1) * 128] = got[p, k * OWN : (k + 1) * OWN, :]
         ups[:, p * HEAD : (p + 1) * HEAD] = got[p, SEND_UP:SEND_RED, :]
+    unpack_rows(got, masked)
     total = got[0, SEND_RED:SEND, :].astype(F32)
     for p in range(1, TENSOR):
         total += got[p, SEND_RED:SEND, :].astype(F32)
@@ -158,13 +204,14 @@
 
 
 def base_kernel(tokens, weight, base):
-    for b in range(BLOCKS):
-        rows = slice(b * BLK, (b + 1) * BLK)
-        base[rows, :] = dot(tokens[rows, :], weight[...], NT).astype(BF16)
-
-
-def input_kernel(idx, pos, masked, weight, low, down, grad):
+    for k in range(Z_HI):
+        columns = slice(k * PLANE, (k + 1) * PLANE)
+        base[:, columns] = dot(tokens[...], weight[columns, :], NT).astype(BF16)
+
+
+def input_kernel(idx, pos, got, weight, low, down, grad, masked):
     data = pos[0]
+    unpack_rows(got, masked)
     for b in range(BLOCKS):
         rows = slice(b * BLK, (b + 1) * BLK)
         adapter = dot(low[b * RANK : (b + 1) * RANK, :], down[idx[data * BLOCKS + b]], TN)
@@ -172,72 +219,86 @@
 
 
 def shards(tokens, value_weight, down, up, value_gradient, block_adapter_index, block_live_rows):
-    same_core = [list(range(core, 2 * PEERS, 2)) for core in range(2)]
-    sibling = [(i, i ^ 1) for i in range(2 * PEERS)]
-    pos = jnp.stack([lax.axis_index("dp"), lax.axis_index("tensor")]).astype(jnp.int32)
+    sibling = [(0, 1), (1, 0)]
+    pos = jnp.stack([lax.axis_index(DP), lax.axis_index(TP)]).astype(jnp.int32)
     idx = block_adapter_index[:, 0]
     live = block_live_rows
     down_t = jnp.swapaxes(down, 1, 2)
-    weight = jnp.swapaxes(lax.all_gather(value_weight, "dp", axis=1, tiled=True), 0, 1)
-
+
+    stripes = jnp.broadcast_to(jnp.swapaxes(value_weight, 0, 1), (Z_HI, STRIPE, WIDTH))
+    stripes = lax.all_to_all(stripes, "z_hi", 0, 0, tiled=True)
     send = call(
         pack_kernel, (idx, live, pos, value_gradient, up, tokens, down_t),
         (out((TENSOR, SEND, 128)),), 2 * ROWS * WIDTH * RANK,
-    )
-    got = lax.all_to_all(send, "tensor", 0, 0, tiled=True)
-    masked, low, mine, theirs, update = call(
+        (
+            pltpu.VMEM((OWN, COLS), BF16),
+            pltpu.VMEM((BLOCKS, RANK, HEAD), BF16),
+            pltpu.VMEM((ROWS, WIDTH), BF16),
+            pltpu.VMEM((BLOCKS, RANK, WIDTH), BF16),
+            pltpu.SemaphoreType.DMA((3 * BLOCKS + 1,)),
+        ),
+        vmem=56, in_place=range(3, 8),
+    )
+    send = after(send, stripes)
+    weight = lax.all_gather(stripes, ("y", "core"), axis=1, tiled=False).reshape(COLS, WIDTH)
+    got = lax.all_to_all(send, TP, 0, 0, tiled=True)
+    low, mine, theirs, update = call(
         terms_kernel, (pos, got, tokens),
-        (out((ROWS, COLS)), out((BLOCKS * RANK, BLK)), out((128, TERM)), out((128, TERM)), out((OWN, COLS), F32)),
+        (out((BLOCKS * RANK, BLK)), out((128, TERM)), out((128, TERM)), out((OWN, COLS), F32)),
         6 * ROWS * WIDTH * RANK,
         (
+            pltpu.VMEM((ROWS, COLS), BF16),
             pltpu.VMEM((BLOCKS * RANK, BLK), BF16),
             pltpu.VMEM((BLOCKS * RANK, COLS), BF16),
             pltpu.VMEM((BLOCKS * RANK, TERM), BF16),
             pltpu.VMEM((BLK, COLS), F32),
         ),
     )
-    theirs = lax.ppermute(theirs, "dp", sibling)
+    theirs = lax.ppermute(theirs, "core", sibling)
     by_peer = call(scatter_kernel, (idx, pos, mine, theirs), (out((PEERS * ADAPTERS, TERM)),), 2 * 256 * 256 * TERM)
-    parts = lax.all_to_all(by_peer, "dp", 0, 0, tiled=True, axis_index_groups=same_core)
+    parts = lax.all_to_all(by_peer, PEER, 0, 0, tiled=True)
+    base = call(base_kernel, (tokens, weight), (out((ROWS, COLS)),), 2 * ROWS * WIDTH * COLS)
+    own_base = lax.psum_scatter(base, TP, scatter_dimension=0, tiled=True)
+    parts, _ = lax.optimization_barrier((parts, base))
     spread = call(
         total_kernel, (idx.reshape(2, 128), live.reshape(2, 128), parts),
         (out((PEERS * ADAPTERS, TERM)),), 256 * TERM,
     )
-    half = lax.all_to_all(spread, "dp", 0, 0, tiled=True, axis_index_groups=same_core)
-    other = lax.ppermute(half, "dp", sibling)
+    half = lax.all_to_all(spread, PEER, 0, 0, tiled=True)
+    input_gradient = call(
+        input_kernel, (idx, pos, got, weight, low, down_t), (out((ROWS, WIDTH)),),
+        2 * ROWS * WIDTH * (COLS + RANK), (pltpu.VMEM((ROWS, COLS), BF16),),
+    )
+    half, input_gradient = lax.optimization_barrier((half, input_gradient))
+    other = lax.ppermute(half, "core", sibling)
     grad_a, grad_b = call(
         unpack_kernel, (pos, half, other),
         (out((ADAPTERS, RANK, WIDTH), F32), out((ADAPTERS, RANK, HEAD), F32)), 4 * 256 * 256 * TERM,
     )
-
-    base = call(base_kernel, (tokens, weight), (out((ROWS, COLS)),), 2 * ROWS * WIDTH * COLS)
-    base_parts = lax.all_to_all(base, "tensor", 0, 0, tiled=True).reshape(TENSOR, OWN, COLS)
-    input_gradient = call(
-        input_kernel, (idx, pos, masked, weight, low, down_t), (out((ROWS, WIDTH)),),
-        2 * ROWS * WIDTH * (COLS + RANK),
-    )
-    values_out = (jnp.sum(base_parts.astype(F32), axis=0) + update).astype(BF16)
+    own_base, grad_b = lax.optimization_barrier((own_base, grad_b))
+    values_out = (own_base.astype(F32) + update).astype(BF16)
     return values_out, input_gradient, jnp.swapaxes(grad_a, 1, 2), grad_b
 
 
 def solution(mesh):
+    grid = Mesh(mesh.devices.reshape(tuple(AXES.values())), tuple(AXES))
     return jax.shard_map(
         shards,
-        mesh=mesh,
+        mesh=grid,
         in_specs=(
-            P("dp", "tensor"),
-            P("tensor", "dp"),
-            P(None, "tensor", None),
-            P(None, None, "tensor"),
-            P(("dp", "tensor"), None),
+            P(DP, TP),
+            P(TP, DP),
+            P(None, TP, None),
+            P(None, None, TP),
+            P((*DP, *TP), None),
             P(),
             P(),
         ),
         out_specs=(
-            P(("dp", "tensor"), None),
-            P("dp", "tensor"),
-            P(None, "tensor", None),
-            P(None, None, "tensor"),
+            P((*DP, *TP), None),
+            P(DP, TP),
+            P(None, TP, None),
+            P(None, None, TP),
         ),
         check_vma=False,
     )

time: 158 us -> 144 us (0.911); the launches traced: 157 us -> 141 us
  blocking collectives: 32.5 us -> 0 us
  starting transfers between devices: 27.2 us -> 42.6 us
  waiting for transfers between devices: 54.6 us -> 58 us
  local copies, waits for them, and re-layouts: 10.7 us -> 7.86 us
    all_to_all x1 -> x0, blocking collectives: 32.5 us -> none  [shards(): lax.all_to_all(by_peer, 'dp', 0, 0, tiled=True, axis_index_groups=same_core)]
    all_to_all x3 -> x4, waiting for transfers between devices: 32.7 us -> 52.4 us  [the longest x1 25.4 us: shards(): got = lax.all_to_all(send, TP, 0, 0, tiled=True)]
    all_gather x1, waiting for transfers between devices: 20 us -> 1.85 us  [shards(): lax.all_gather(stripes, ('y', 'core'), axis=1, tiled=False)]
    all_to_all x3 -> x4, starting transfers between devices: 21 us -> 33.8 us  [the longest x1 10.8 us: shards(): stripes = lax.all_to_all(stripes, 'z_hi', 0, 0, tiled=True)]
    unnamed x30 -> x22, local copies, waits for them, and re-layouts: 10.7 us -> 6.44 us
    ppermute x2, starting transfers between devices: 6.17 us -> 8.69 us  [the longest x1 5.94 us: shards(): other = lax.ppermute(half, 'core', sibling)]
    ppermute x2, waiting for transfers between devices: 1.19 us -> 3.05 us  [the longest x1 1.82 us: shards(): other = lax.ppermute(half, 'core', sibling)]
  transfers between devices with their start and end apart: 6 -> 8, of which waited for: 4 -> 7; matrix products, arithmetic and copies ran while one was open for 1% -> 0% of each run, Pallas kernels for 7% -> 12%
where the time goes in v2:
time: 144 us; the launch traced here: 141 us
  waiting for transfers between devices  58 us (40%)
  starting transfers between devices  42.6 us (30%)
  Pallas kernels  16.5 us (11%)
  between operations  14.2 us (10%)
  local copies, waits for them, and re-layouts  7.86 us (5%)
  other arithmetic  2.2 us (2%)
    all_to_all x1, waiting for transfers between devices, shards(): got = lax.all_to_all(send, TP, 0, 0, tiled=True)  25.4 us
    pallas_call x7, Pallas kernels, call(): pl.pallas_call(kernel, out_shape=tuple(outs) if many else outs[0], in_spe...  16.5 us
    all_to_all x1, waiting for transfers between devices, shards(): half = lax.all_to_all(spread, PEER, 0, 0, tiled=True)  12.3 us
    all_to_all x1, waiting for transfers between devices, shards(): parts = lax.all_to_all(by_peer, PEER, 0, 0, tiled=True)  12.2 us
    all_to_all x1, starting transfers between devices, shards(): stripes = lax.all_to_all(stripes, 'z_hi', 0, 0, tiled=True)  10.8 us
    all_to_all x1, starting transfers between devices, shards(): parts = lax.all_to_all(by_peer, PEER, 0, 0, tiled=True)  9.83 us
    all_to_all x1, starting transfers between devices, shards(): half = lax.all_to_all(spread, PEER, 0, 0, tiled=True)  8.13 us
    unnamed x22, local copies, waits for them, and re-layouts  6.44 us
  transfers between devices with their start and end apart: 8, of which 7 were waited for; matrix products, arithmetic and copies ran while one was open for 0% of the time, Pallas kernels for 12%

profile of v2, /device:TPU:1, one launch (start us, length us, event | category | flops | bytes accessed | tf_op | source)
XLA Modules:
  0.0 141.4 jit_solution(1355179384399575393)
XLA Ops:
  7.2 1.4 %broadcast_in_dim.3 = bf16[4,16,1024]{2,1,0:T(8,128)(2,1)} broadcast(bf16[16,1024]{1,0:T(8,128)(2,1)} %bitcast.24), dimensions={1,2} | broadcast | bytes 163840 | tf_op jit(solution)/shard_map/broadcast_in_dim | solution.py:228
  8.6 10.8 %all-to-all-start = ((bf16[4,16,1024]{2,1,0:T(8,128)(2,1)}), bf16[4,16,1024]{2,1,0:T(8,128)(2,1)S(1)}, u32[]{:S(2)}, u32[]{:S(2)}) async-start(bf16[4,16,1024]{2,1,0:T(8,128)(2,1)} %broadcast_in_dim.3), calls=%async_computation | async-start | bytes 262144 | tf_op jit(solution)/shard_map/all_to_all | solution.py:229
  20.0 4.3 %shard_map.103.value_in = bf16[8,1024,128]{2,1,0:T(8,128)(2,1)} custom-call(s32[256]{0:T(256)} %bitcast.19, s32[256]{0:T(256)} %live.1, s32[2]{0:T(128)} %pad_add_fusion.pos, bf16[64,1024]{1,0:T(8,128)(2,1)} %grad_in.1, bf16[8,64,128]{2,1,0:T(8,128)(2,1)} %up_in.1, bf16[512,1024]{1,0:T(8,128)(2,1)} %tokens.3, bf16[8,64,1024]{2,1,0:T(8,128)(2,1)} %bitcast.15), custom_call_target="tpu_custom_call" | custom-call | flops 67108864 | bytes 4458504 | tf_op jit(solution)/shard_map/pallas_call | solution.py:46
  24.4 2.6 %all-to-all-done.earlier_in = bf16[4,16,1024]{2,1,0:T(8,128)(2,1)S(1)} async-done(((bf16[4,16,1024]{2,1,0:T(8,128)(2,1)}), bf16[4,16,1024]{2,1,0:T(8,128)(2,1)S(1)}, u32[]{:S(2)}, u32[]{:S(2)}) %all-to-all-start) | async-done | bytes 131104 | tf_op jit(solution)/shard_map/all_to_all | solution.py:229
  27.7 5.0 %all-to-all-start.1 = ((bf16[8,1024,128]{2,1,0:T(8,128)(2,1)}), bf16[8,1024,128]{2,1,0:T(8,128)(2,1)S(1)}, u32[]{:S(2)}, u32[]{:S(2)}) async-start(bf16[8,1024,128]{2,1,0:T(8,128)(2,1)} %shard_map.104), calls=%async_computation.2 | async-start | bytes 4194304 | tf_op jit(solution)/shard_map/all_to_all | solution.py:244
  33.4 25.4 %all-to-all-done.1.got = bf16[8,1024,128]{2,1,0:T(8,128)(2,1)S(1)} async-done(((bf16[8,1024,128]{2,1,0:T(8,128)(2,1)}), bf16[8,1024,128]{2,1,0:T(8,128)(2,1)S(1)}, u32[]{:S(2)}, u32[]{:S(2)}) %all-to-all-start.1) | async-done | bytes 2097184 | tf_op jit(solution)/shard_map/all_to_all | solution.py:244
  58.8 2.2 %shard_map.105 = (bf16[256,128]{1,0:T(8,128)(2,1)S(1)}, bf16[128,1152]{1,0:T(8,128)(2,1)S(1)}, bf16[128,1152]{1,0:T(8,128)(2,1)S(1)}, f32[64,1024]{1,0:T(8,128)S(1)}) custom-call(s32[2]{0:T(128)S(1)} %copy-done.8, bf16[8,1024,128]{2,1,0:T(8,128)(2,1)S(1)} %all-to-all-done.1.got, bf16[512,1024]{1,0:T(8,128)(2,1)S(1)} %copy-done), custom_call_target="tpu_custom_call" | custom-call | flops 201326592 | bytes 4063240 | tf_op jit(solution)/shard_map/pallas_call | solution.py:46
  61.1 2.7 %collective-permute-start = (bf16[128,1152]{1,0:T(8,128)(2,1)S(1)}, bf16[128,1152]{1,0:T(8,128)(2,1)S(1)}, u32[]{:S(2)}, u32[]{:S(2)}) collective-permute-start(bf16[128,1152]{1,0:T(8,128)(2,1)S(1)} %get-tuple-element.16), channel_id=1, source_target_pairs={{0,8},{8,0},{1,9},{9,1},{2,10},{10,2},{3,11},{11,3},{4,12},{12,4},... | collective-permute-start | bytes 884744 | tf_op jit(solution)/shard_map/ppermute | solution.py:257
  63.8 1.2 collective-permute-done.theirs
  65.1 1.0 shard_map.106
  66.9 9.8 %all-to-all-start.2 = ((bf16[32,8,1152]{2,1,0:T(8,128)(2,1)}), bf16[32,8,1152]{2,1,0:T(8,128)(2,1)}, u32[]{:S(2)}, u32[]{:S(2)}) async-start(bf16[32,8,1152]{2,1,0:T(8,128)(2,1)} %bitcast.17), calls=%async_computation.3 | async-start | bytes 1179648 | tf_op jit(solution)/shard_map/all_to_all | solution.py:259
  76.8 1.9 %all-gather.3.cloned.1.call-done = bf16[4,256,1024]{2,1,0:T(8,128)(2,1)} async-done(((bf16[4,16,1024]{2,1,0:T(8,128)(2,1)}), bf16[4,256,1024]{2,1,0:T(8,128)(2,1)}) %all-gather.3.cloned.1.call-update) | async-done | bytes 2097168 | tf_op jit(solution)/shard_map/all_gather | solution.py:243
  78.6 1.6 %copy-done.1 = bf16[4,256,1024]{2,1,0:T(8,128)(2,1)S(1)} copy-done((bf16[4,256,1024]{2,1,0:T(8,128)(2,1)S(1)}, bf16[4,256,1024]{2,1,0:T(8,128)(2,1)}, u32[]{:S(2)}) %copy-start.1) | copy-done | bytes 2097176
  80.2 1.3 shard_map.102
  82.5 12.2 %all-to-all-done.2 = bf16[32,8,1152]{2,1,0:T(8,128)(2,1)} async-done(((bf16[32,8,1152]{2,1,0:T(8,128)(2,1)}), bf16[32,8,1152]{2,1,0:T(8,128)(2,1)}, u32[]{:S(2)}, u32[]{:S(2)}) %all-to-all-start.2) | async-done | bytes 589856 | tf_op jit(solution)/shard_map/all_to_all | solution.py:259
  94.7 1.3 shard_map.107
  96.8 8.1 %all-to-all-start.3 = ((bf16[32,8,1152]{2,1,0:T(8,128)(2,1)}), bf16[32,8,1152]{2,1,0:T(8,128)(2,1)}, u32[]{:S(2)}, u32[]{:S(2)}) async-start(bf16[32,8,1152]{2,1,0:T(8,128)(2,1)} %bitcast.18), calls=%async_computation.4 | async-start | bytes 1179648 | tf_op jit(solution)/shard_map/all_to_all | solution.py:267
  105.0 1.6 %copy-done.2 = bf16[4,256,1024]{2,1,0:T(8,128)(2,1)S(1)} copy-done((bf16[4,256,1024]{2,1,0:T(8,128)(2,1)S(1)}, bf16[4,256,1024]{2,1,0:T(8,128)(2,1)}, u32[]{:S(2)}) %copy-start.2) | copy-done | bytes 2097176
  106.6 3.1 %shard_map.108 = bf16[512,1024]{1,0:T(8,128)(2,1)} custom-call(s32[256]{0:T(256)S(1)} %bitcast.22, s32[2]{0:T(128)S(1)} %copy-done.8, bf16[8,1024,128]{2,1,0:T(8,128)(2,1)S(1)} %all-to-all-done.1.got, bf16[1024,1024]{1,0:T(8,128)(2,1)S(1)} %bitcast.14, bf16[256,128]{1,0:T(8,128)(2,1)S(1)} %get-tuple-element.18.low, bf16[8,64,1024]{2,1,0:T(8,128)(2,1)S(1)} %bitcast.16), custom_call_target="tpu_custom_call" | custom-call | flops 1140850688 | bytes 6358024 | tf_op jit(solution)/shard_map/pallas_call | solution.py:46
  109.7 12.3 %all-to-all-done.3 = bf16[32,8,1152]{2,1,0:T(8,128)(2,1)} async-done(((bf16[32,8,1152]{2,1,0:T(8,128)(2,1)}), bf16[32,8,1152]{2,1,0:T(8,128)(2,1)}, u32[]{:S(2)}, u32[]{:S(2)}) %all-to-all-start.3) | async-done | bytes 589856 | tf_op jit(solution)/shard_map/all_to_all | solution.py:267
  122.0 5.9 %collective-permute-start.1 = (bf16[256,1152]{1,0:T(8,128)(2,1)}, bf16[256,1152]{1,0:T(8,128)(2,1)S(1)}, u32[]{:S(2)}, u32[]{:S(2)}) collective-permute-start(bf16[256,1152]{1,0:T(8,128)(2,1)} %bitcast.11.mine), channel_id=1, source_target_pairs={{0,8},{8,0},{1,9},{9,1},{2,10},{10,2},{3,11},{11,3},{4,12},{12,4},... | collective-permute-start | bytes 1769480 | tf_op jit(solution)/shard_map/ppermute | solution.py:273
  127.9 1.8 %collective-permute-done.1.theirs = bf16[256,1152]{1,0:T(8,128)(2,1)S(1)} collective-permute-done((bf16[256,1152]{1,0:T(8,128)(2,1)}, bf16[256,1152]{1,0:T(8,128)(2,1)S(1)}, u32[]{:S(2)}, u32[]{:S(2)}) %collective-permute-start.1) | collective-permute-done | bytes 589856 | tf_op jit(solution)/shard_map/ppermute | solution.py:273
  129.8 3.2 %shard_map.109 = (f32[8,64,1024]{2,1,0:T(8,128)}, f32[8,64,128]{2,1,0:T(8,128)}) custom-call(s32[2]{0:T(128)S(1)} %copy-done.8, bf16[256,1152]{1,0:T(8,128)(2,1)} %bitcast.11.mine, bf16[256,1152]{1,0:T(8,128)(2,1)S(1)} %collective-permute-done.1.theirs), custom_call_target="tpu_custom_call" | custom-call | flops 301989888 | bytes 3538952 | tf_op jit(solution)/shard_map/pallas_call | solution.py:46
  133.0 1.6 %add_convert_fusion = bf16[64,1024]{1,0:T(8,128)(2,1)} fusion(f32[64,1024]{1,0:T(8,128)S(1)} %get-tuple-element.22, bf16[64,1024]{1,0:T(8,128)(2,1)} %reduce-scatter.2.cloned.1.call-done), kind=kLoop, calls=%fused_computation | loop fusion | flops 196608 | bytes 524288 | tf_op jit(solution)/shard_map/convert_element_type | solution.py:279
  (27 shorter events, 4.7 us)
Async XLA Ops:
  8.6 18.4 %all-to-all-start = ((bf16[4,16,1024]{2,1,0:T(8,128)(2,1)}), bf16[4,16,1024]{2,1,0:T(8,128)(2,1)S(1)}, u32[]{:S(2)}, u32[]{:S(2)}) async-start(bf16[4,16,1024]{2,1,0:T(8,128)(2,1)} %broadcast_in_dim.3), calls=%async_computation | async-start | bytes 262144 | tf_op jit(solution)/shard_map/all_to_all | solution.py:229
  27.0 0.7 copy-start.10
  27.7 31.2 %copy-start = (bf16[512,1024]{1,0:T(8,128)(2,1)S(1)}, bf16[512,1024]{1,0:T(8,128)(2,1)}, u32[]{:S(2)}) copy-start(bf16[512,1024]{1,0:T(8,128)(2,1)} %tokens.3) | copy-start | bytes 3145732
  27.7 31.2 %copy-start.8 = (s32[2]{0:T(128)S(1)}, s32[2]{0:T(128)}, u32[]{:S(2)}) copy-start(s32[2]{0:T(128)} %pad_add_fusion.pos) | copy-start | bytes 28
  27.7 31.2 %all-to-all-start.1 = ((bf16[8,1024,128]{2,1,0:T(8,128)(2,1)}), bf16[8,1024,128]{2,1,0:T(8,128)(2,1)S(1)}, u32[]{:S(2)}, u32[]{:S(2)}) async-start(bf16[8,1024,128]{2,1,0:T(8,128)(2,1)} %shard_map.104), calls=%async_computation.2 | async-start | bytes 4194304 | tf_op jit(solution)/shard_map/all_to_all | solution.py:244
  32.7 32.4 %copy-start.7 = (s32[256,1]{0,1:T(1,128)S(1)}, s32[256,1]{0,1:T(1,128)}, u32[]{:S(2)}) copy-start(s32[256,1]{0,1:T(1,128)} %param.12) | copy-start | bytes 3076
  32.7 45.9 %all-gather.3.cloned.1.call-start = ((), (), s32[]{:S(2)}) async-start(), calls=%async_computation.6 | async-start | bytes 2228224 | tf_op jit(solution)/shard_map/all_gather | solution.py:243
  61.1 4.0 %collective-permute-start = (bf16[128,1152]{1,0:T(8,128)(2,1)S(1)}, bf16[128,1152]{1,0:T(8,128)(2,1)S(1)}, u32[]{:S(2)}, u32[]{:S(2)}) collective-permute-start(bf16[128,1152]{1,0:T(8,128)(2,1)S(1)} %get-tuple-element.16), channel_id=1, source_target_pairs={{0,8},{8,0},{1,9},{9,1},{2,10},{10,2},{3,11},{11,3},{4,12},{12,4},... | collective-permute-start | bytes 884744 | tf_op jit(solution)/shard_map/ppermute | solution.py:257
  66.1 0.8 copy-start.5
  66.9 27.8 %all-to-all-start.2 = ((bf16[32,8,1152]{2,1,0:T(8,128)(2,1)}), bf16[32,8,1152]{2,1,0:T(8,128)(2,1)}, u32[]{:S(2)}, u32[]{:S(2)}) async-start(bf16[32,8,1152]{2,1,0:T(8,128)(2,1)} %bitcast.17), calls=%async_computation.3 | async-start | bytes 1179648 | tf_op jit(solution)/shard_map/all_to_all | solution.py:259
  76.7 56.3 %reduce-scatter.2.cloned.1.call-start = ((), (), s32[]{:S(2)}) async-start(), calls=%async_computation.5 | async-start | bytes 1179648 | tf_op jit(solution)/shard_map/reduce_scatter | solution.py:261
  78.6 1.6 %copy-start.1 = (bf16[4,256,1024]{2,1,0:T(8,128)(2,1)S(1)}, bf16[4,256,1024]{2,1,0:T(8,128)(2,1)}, u32[]{:S(2)}) copy-start(bf16[4,256,1024]{2,1,0:T(8,128)(2,1)} %all-gather.3.cloned.1.call-done) | copy-start | bytes 6291460
  80.2 14.5 %copy-start.9 = (s32[256]{0:T(256)S(1)}, s32[256]{0:T(256)}, u32[]{:S(2)}) copy-start(s32[256]{0:T(256)} %live.1) | copy-start | bytes 3076
  81.5 1.0 copy-start.3
  82.5 22.5 %copy-start.4 = (bf16[8,1024,64]{1,2,0:T(8,128)(2,1)S(1)}, bf16[8,1024,64]{1,2,0:T(8,128)(2,1)}, u32[]{:S(2)}) copy-start(bf16[8,1024,64]{1,2,0:T(8,128)(2,1)} %param.9) | copy-start | bytes 3145732
  96.0 0.8 copy-start.6
  96.8 25.2 %all-to-all-start.3 = ((bf16[32,8,1152]{2,1,0:T(8,128)(2,1)}), bf16[32,8,1152]{2,1,0:T(8,128)(2,1)}, u32[]{:S(2)}, u32[]{:S(2)}) async-start(bf16[32,8,1152]{2,1,0:T(8,128)(2,1)} %bitcast.18), calls=%async_computation.4 | async-start | bytes 1179648 | tf_op jit(solution)/shard_map/all_to_all | solution.py:267
  105.0 1.6 %copy-start.2 = (bf16[4,256,1024]{2,1,0:T(8,128)(2,1)S(1)}, bf16[4,256,1024]{2,1,0:T(8,128)(2,1)}, u32[]{:S(2)}) copy-start(bf16[4,256,1024]{2,1,0:T(8,128)(2,1)} %all-gather.3.cloned.1.call-done) | copy-start | bytes 6291460
  122.0 7.8 %collective-permute-start.1 = (bf16[256,1152]{1,0:T(8,128)(2,1)}, bf16[256,1152]{1,0:T(8,128)(2,1)S(1)}, u32[]{:S(2)}, u32[]{:S(2)}) collective-permute-start(bf16[256,1152]{1,0:T(8,128)(2,1)} %bitcast.11.mine), channel_id=1, source_target_pairs={{0,8},{8,0},{1,9},{9,1},{2,10},{10,2},{3,11},{11,3},{4,12},{12,4},... | collective-permute-start | bytes 1769480 | tf_op jit(solution)/shard_map/ppermute | solution.py:273
Sparse Core Ops, SparseCore 0:
  36.3 42.3 all-gather.2
  82.6 46.2 reduce-scatter.1

commit v3 on v2

--- a/solution.py
+++ b/solution.py
@@ -65,19 +65,8 @@
     return lax.dot_general(a, b, dims, preferred_element_type=F32)
 
 
-def after(value, earlier):
-    return pl.pallas_call(
-        lambda value_in, earlier_in, value_out: None,
-        out_shape=out(value.shape, value.dtype),
-        in_specs=[ANY, ANY],
-        out_specs=ANY,
-        input_output_aliases={0: 0},
-        cost_estimate=pl.CostEstimate(flops=0, bytes_accessed=0, transcendentals=0),
-    )(value, earlier)
-
-
-def pack_kernel(idx, live, pos, grad_in, up_in, tokens_in, down_in, send, grad, up, tokens, down, sems):
-    data, tensor = pos[0], pos[1]
+def pack_kernel(idx, live, grad_in, up_in, tokens_in, down_in, send, grad, up, tokens, down, sems):
+    data, tensor = lax.axis_index(DP), lax.axis_index(TP)
     copies = []
     for b in range(BLOCKS):
         a = idx[data * BLOCKS + b]
@@ -119,8 +108,8 @@
             masked[p * OWN : (p + 1) * OWN, k * 128 : (k + 1) * 128] = got[p, k * OWN : (k + 1) * OWN, :]
 
 
-def terms_kernel(pos, got, tokens, low, mine, theirs, update, masked, red, ups, terms, block_update):
-    data, tensor = pos[0], pos[1]
+def terms_kernel(got, tokens, low, mine, theirs, update, masked, red, ups, terms, block_update):
+    data, tensor = lax.axis_index(DP), lax.axis_index(TP)
     core = data % 2
     for p in range(TENSOR):
         ups[:, p * HEAD : (p + 1) * HEAD] = got[p, SEND_UP:SEND_RED, :]
@@ -148,8 +137,8 @@
     update[...] = block_update[pl.ds(pl.multiple_of((tensor % 2) * OWN, OWN), OWN), :]
 
 
-def scatter_kernel(idx, pos, mine, theirs, by_peer):
-    data = pos[0]
+def scatter_kernel(idx, mine, theirs, by_peer):
+    data = lax.axis_index(DP)
     row = lax.broadcasted_iota(jnp.int32, (PEERS * ADAPTERS, 128), 0)
     column = lax.broadcasted_iota(jnp.int32, (PEERS * ADAPTERS, 128), 1)
 
@@ -185,8 +174,8 @@
             spread[p * 16 : (p + 1) * 16, lanes] = both
 
 
-def unpack_kernel(pos, mine, theirs, grad_a, grad_b):
-    core = pos[0] % 2
+def unpack_kernel(mine, theirs, grad_a, grad_b):
+    core = lax.axis_index(DP) % 2
     row = lax.broadcasted_iota(jnp.int32, (256, 256), 0)
     column = lax.broadcasted_iota(jnp.int32, (256, 256), 1)
     order = jnp.where(column == (row % PEERS) * ADAPTERS + row // PEERS, 1.0, 0.0).astype(BF16)
@@ -209,8 +198,8 @@
         base[:, columns] = dot(tokens[...], weight[columns, :], NT).astype(BF16)
 
 
-def input_kernel(idx, pos, got, weight, low, down, grad, masked):
-    data = pos[0]
+def input_kernel(idx, got, weight, low, down, grad, masked):
+    data = lax.axis_index(DP)
     unpack_rows(got, masked)
     for b in range(BLOCKS):
         rows = slice(b * BLK, (b + 1) * BLK)
@@ -220,7 +209,6 @@
 
 def shards(tokens, value_weight, down, up, value_gradient, block_adapter_index, block_live_rows):
     sibling = [(0, 1), (1, 0)]
-    pos = jnp.stack([lax.axis_index(DP), lax.axis_index(TP)]).astype(jnp.int32)
     idx = block_adapter_index[:, 0]
     live = block_live_rows
     down_t = jnp.swapaxes(down, 1, 2)
@@ -228,7 +216,7 @@
     stripes = jnp.broadcast_to(jnp.swapaxes(value_weight, 0, 1), (Z_HI, STRIPE, WIDTH))
     stripes = lax.all_to_all(stripes, "z_hi", 0, 0, tiled=True)
     send = call(
-        pack_kernel, (idx, live, pos, value_gradient, up, tokens, down_t),
+        pack_kernel, (idx, live, value_gradient, up, tokens, down_t),
         (out((TENSOR, SEND, 128)),), 2 * ROWS * WIDTH * RANK,
         (
             pltpu.VMEM((OWN, COLS), BF16),
@@ -237,13 +225,12 @@
             pltpu.VMEM((BLOCKS, RANK, WIDTH), BF16),
             pltpu.SemaphoreType.DMA((3 * BLOCKS + 1,)),
         ),
-        vmem=56, in_place=range(3, 8),
-    )
-    send = after(send, stripes)
+        vmem=56, in_place=range(2, 6),
+    )
     weight = lax.all_gather(stripes, ("y", "core"), axis=1, tiled=False).reshape(COLS, WIDTH)
     got = lax.all_to_all(send, TP, 0, 0, tiled=True)
     low, mine, theirs, update = call(
-        terms_kernel, (pos, got, tokens),
+        terms_kernel, (got, tokens),
         (out((BLOCKS * RANK, BLK)), out((128, TERM)), out((128, TERM)), out((OWN, COLS), F32)),
         6 * ROWS * WIDTH * RANK,
         (
@@ -255,7 +242,7 @@
         ),
     )
     theirs = lax.ppermute(theirs, "core", sibling)
-    by_peer = call(scatter_kernel, (idx, pos, mine, theirs), (out((PEERS * ADAPTERS, TERM)),), 2 * 256 * 256 * TERM)
+    by_peer = call(scatter_kernel, (idx, mine, theirs), (out((PEERS * ADAPTERS, TERM)),), 2 * 256 * 256 * TERM)
     parts = lax.all_to_all(by_peer, PEER, 0, 0, tiled=True)
     base = call(base_kernel, (tokens, weight), (out((ROWS, COLS)),), 2 * ROWS * WIDTH * COLS)
     own_base = lax.psum_scatter(base, TP, scatter_dimension=0, tiled=True)
@@ -266,13 +253,13 @@
     )
     half = lax.all_to_all(spread, PEER, 0, 0, tiled=True)
     input_gradient = call(
-        input_kernel, (idx, pos, got, weight, low, down_t), (out((ROWS, WIDTH)),),
+        input_kernel, (idx, got, weight, low, down_t), (out((ROWS, WIDTH)),),
         2 * ROWS * WIDTH * (COLS + RANK), (pltpu.VMEM((ROWS, COLS), BF16),),
     )
     half, input_gradient = lax.optimization_barrier((half, input_gradient))
     other = lax.ppermute(half, "core", sibling)
     grad_a, grad_b = call(
-        unpack_kernel, (pos, half, other),
+        unpack_kernel, (half, other),
         (out((ADAPTERS, RANK, WIDTH), F32), out((ADAPTERS, RANK, HEAD), F32)), 4 * 256 * 256 * TERM,
     )
     own_base, grad_b = lax.optimization_barrier((own_base, grad_b))

time: 144 us -> 145 us (level)
  the two profiles are of different devices: /device:TPU:1 before, /device:TPU:32 now
where the time goes in v3:
time: 145 us; the launch traced here: 144 us
  waiting for transfers between devices  68.3 us (47%)
  starting transfers between devices  36.3 us (25%)
  Pallas kernels  16 us (11%)
  between operations  14.2 us (10%)
  local copies, waits for them, and re-layouts  7.86 us (5%)
  other arithmetic  1.58 us (1%)
    all_to_all x1, waiting for transfers between devices, shards(): got = lax.all_to_all(send, TP, 0, 0, tiled=True)  24.2 us
    pallas_call x7, Pallas kernels, call(): pl.pallas_call(kernel, out_shape=tuple(outs) if many else outs[0], in_spe...  16 us
    all_to_all x1, waiting for transfers between devices, shards(): parts = lax.all_to_all(by_peer, PEER, 0, 0, tiled=True)  14.5 us
    all_to_all x1, waiting for transfers between devices, shards(): half = lax.all_to_all(spread, PEER, 0, 0, tiled=True)  13.9 us
    all_to_all x1, starting transfers between devices, shards(): stripes = lax.all_to_all(stripes, 'z_hi', 0, 0, tiled=True)  10.3 us
    all_to_all x1, starting transfers between devices, shards(): parts = lax.all_to_all(by_peer, PEER, 0, 0, tiled=True)  9.32 us
    all_to_all x1, starting transfers between devices, shards(): half = lax.all_to_all(spread, PEER, 0, 0, tiled=True)  8.43 us
    unnamed x20, local copies, waits for them, and re-layouts  6.44 us
  transfers between devices with their start and end apart: 8, of which 7 were waited for; matrix products, arithmetic and copies ran while one was open for 0% of the time, Pallas kernels for 11%

profile of v3, /device:TPU:32, one launch (start us, length us, event | category | flops | bytes accessed | tf_op | source)
XLA Modules:
  0.0 144.2 jit_solution(15527769466351131382)
XLA Ops:
  7.2 1.4 broadcast_in_dim.3
  8.6 10.3 %all-to-all-start = ((bf16[4,16,1024]{2,1,0:T(8,128)(2,1)}), bf16[4,16,1024]{2,1,0:T(8,128)(2,1)S(1)}, u32[]{:S(2)}, u32[]{:S(2)}) async-start(bf16[4,16,1024]{2,1,0:T(8,128)(2,1)} %broadcast_in_dim.3), calls=%async_computation | async-start | bytes 262144 | tf_op jit(solution)/shard_map/all_to_all | solution.py:217
  18.9 4.3 %shard_map.103 = bf16[8,1024,128]{2,1,0:T(8,128)(2,1)} custom-call(s32[256]{0:T(256)} %bitcast.17, s32[256]{0:T(256)} %live.1, bf16[64,1024]{1,0:T(8,128)(2,1)} %grad_in.1, bf16[8,64,128]{2,1,0:T(8,128)(2,1)} %up_in.1, bf16[512,1024]{1,0:T(8,128)(2,1)} %tokens.3, bf16[8,64,1024]{2,1,0:T(8,128)(2,1)} %bitcast.13), custom_call_target="tpu_custom_call" | custom-call | flops 67108864 | bytes 4458496 | tf_op jit(solution)/shard_map/pallas_call | solution.py:46
  23.2 4.9 %all-to-all-done = bf16[4,16,1024]{2,1,0:T(8,128)(2,1)S(1)} async-done(((bf16[4,16,1024]{2,1,0:T(8,128)(2,1)}), bf16[4,16,1024]{2,1,0:T(8,128)(2,1)S(1)}, u32[]{:S(2)}, u32[]{:S(2)}) %all-to-all-start) | async-done | bytes 131104 | tf_op jit(solution)/shard_map/all_to_all | solution.py:217
  28.8 4.3 %all-to-all-start.1 = ((bf16[8,1024,128]{2,1,0:T(8,128)(2,1)}), bf16[8,1024,128]{2,1,0:T(8,128)(2,1)S(1)}, u32[]{:S(2)}, u32[]{:S(2)}) async-start(bf16[8,1024,128]{2,1,0:T(8,128)(2,1)} %shard_map.103), calls=%async_computation.2 | async-start | bytes 4194304 | tf_op jit(solution)/shard_map/all_to_all | solution.py:231
  33.9 24.2 %all-to-all-done.1.got = bf16[8,1024,128]{2,1,0:T(8,128)(2,1)S(1)} async-done(((bf16[8,1024,128]{2,1,0:T(8,128)(2,1)}), bf16[8,1024,128]{2,1,0:T(8,128)(2,1)S(1)}, u32[]{:S(2)}, u32[]{:S(2)}) %all-to-all-start.1) | async-done | bytes 2097184 | tf_op jit(solution)/shard_map/all_to_all | solution.py:231
  58.0 1.7 %shard_map.104 = (bf16[256,128]{1,0:T(8,128)(2,1)S(1)}, bf16[128,1152]{1,0:T(8,128)(2,1)S(1)}, bf16[128,1152]{1,0:T(8,128)(2,1)S(1)}, f32[64,1024]{1,0:T(8,128)S(1)}) custom-call(bf16[8,1024,128]{2,1,0:T(8,128)(2,1)S(1)} %all-to-all-done.1.got, bf16[512,1024]{1,0:T(8,128)(2,1)S(1)} %copy-done), custom_call_target="tpu_custom_call" | custom-call | flops 201326592 | bytes 4063232 | tf_op jit(solution)/shard_map/pallas_call | solution.py:46
  59.7 1.9 %collective-permute-start = (bf16[128,1152]{1,0:T(8,128)(2,1)S(1)}, bf16[128,1152]{1,0:T(8,128)(2,1)S(1)}, u32[]{:S(2)}, u32[]{:S(2)}) collective-permute-start(bf16[128,1152]{1,0:T(8,128)(2,1)S(1)} %get-tuple-element.16), channel_id=1, source_target_pairs={{0,8},{8,0},{1,9},{9,1},{2,10},{10,2},{3,11},{11,3},{4,12},{12,4},... | collective-permute-start | bytes 884744 | tf_op jit(solution)/shard_map/ppermute | solution.py:244
  61.6 1.5 %collective-permute-done.theirs = bf16[128,1152]{1,0:T(8,128)(2,1)S(1)} collective-permute-done((bf16[128,1152]{1,0:T(8,128)(2,1)S(1)}, bf16[128,1152]{1,0:T(8,128)(2,1)S(1)}, u32[]{:S(2)}, u32[]{:S(2)}) %collective-permute-start) | collective-permute-done | bytes 294944 | tf_op jit(solution)/shard_map/ppermute | solution.py:244
  63.2 1.0 shard_map.105
  65.0 9.3 %all-to-all-start.2 = ((bf16[32,8,1152]{2,1,0:T(8,128)(2,1)}), bf16[32,8,1152]{2,1,0:T(8,128)(2,1)}, u32[]{:S(2)}, u32[]{:S(2)}) async-start(bf16[32,8,1152]{2,1,0:T(8,128)(2,1)} %bitcast.15), calls=%async_computation.3 | async-start | bytes 1179648 | tf_op jit(solution)/shard_map/all_to_all | solution.py:246
  74.4 1.6 %copy-done.1 = bf16[4,256,1024]{2,1,0:T(8,128)(2,1)S(1)} copy-done((bf16[4,256,1024]{2,1,0:T(8,128)(2,1)S(1)}, bf16[4,256,1024]{2,1,0:T(8,128)(2,1)}, u32[]{:S(2)}) %copy-start.1) | copy-done | bytes 2097176
  76.0 1.3 shard_map.102
  78.3 14.5 %all-to-all-done.2 = bf16[32,8,1152]{2,1,0:T(8,128)(2,1)} async-done(((bf16[32,8,1152]{2,1,0:T(8,128)(2,1)}), bf16[32,8,1152]{2,1,0:T(8,128)(2,1)}, u32[]{:S(2)}, u32[]{:S(2)}) %all-to-all-start.2) | async-done | bytes 589856 | tf_op jit(solution)/shard_map/all_to_all | solution.py:246
  92.8 1.3 shard_map.106
  94.9 8.4 %all-to-all-start.3 = ((bf16[32,8,1152]{2,1,0:T(8,128)(2,1)}), bf16[32,8,1152]{2,1,0:T(8,128)(2,1)}, u32[]{:S(2)}, u32[]{:S(2)}) async-start(bf16[32,8,1152]{2,1,0:T(8,128)(2,1)} %bitcast.16), calls=%async_computation.4 | async-start | bytes 1179648 | tf_op jit(solution)/shard_map/all_to_all | solution.py:254
  103.4 1.6 %copy-done.2 = bf16[4,256,1024]{2,1,0:T(8,128)(2,1)S(1)} copy-done((bf16[4,256,1024]{2,1,0:T(8,128)(2,1)S(1)}, bf16[4,256,1024]{2,1,0:T(8,128)(2,1)}, u32[]{:S(2)}) %copy-start.2) | copy-done | bytes 2097176
  105.0 3.2 %shard_map.107 = bf16[512,1024]{1,0:T(8,128)(2,1)} custom-call(s32[256]{0:T(256)S(1)} %bitcast.20, bf16[8,1024,128]{2,1,0:T(8,128)(2,1)S(1)} %all-to-all-done.1.got, bf16[1024,1024]{1,0:T(8,128)(2,1)S(1)} %bitcast.12, bf16[256,128]{1,0:T(8,128)(2,1)S(1)} %get-tuple-element.18.low, bf16[8,64,1024]{2,1,0:T(8,128)(2,1)S(1)} %bitcast.14), custom_call_target="tpu_custom_call" | custom-call | flops 1140850688 | bytes 6358016 | tf_op jit(solution)/shard_map/pallas_call | solution.py:46
  108.2 13.9 %all-to-all-done.3 = bf16[32,8,1152]{2,1,0:T(8,128)(2,1)} async-done(((bf16[32,8,1152]{2,1,0:T(8,128)(2,1)}), bf16[32,8,1152]{2,1,0:T(8,128)(2,1)}, u32[]{:S(2)}, u32[]{:S(2)}) %all-to-all-start.3) | async-done | bytes 589856 | tf_op jit(solution)/shard_map/all_to_all | solution.py:254
  122.1 1.9 %collective-permute-start.1 = (bf16[256,1152]{1,0:T(8,128)(2,1)}, bf16[256,1152]{1,0:T(8,128)(2,1)S(1)}, u32[]{:S(2)}, u32[]{:S(2)}) collective-permute-start(bf16[256,1152]{1,0:T(8,128)(2,1)} %bitcast.9.mine), channel_id=1, source_target_pairs={{0,8},{8,0},{1,9},{9,1},{2,10},{10,2},{3,11},{11,3},{4,12},{12,4},... | collective-permute-start | bytes 1769480 | tf_op jit(solution)/shard_map/ppermute | solution.py:260
  124.0 2.2 %collective-permute-done.1.theirs = bf16[256,1152]{1,0:T(8,128)(2,1)S(1)} collective-permute-done((bf16[256,1152]{1,0:T(8,128)(2,1)}, bf16[256,1152]{1,0:T(8,128)(2,1)S(1)}, u32[]{:S(2)}, u32[]{:S(2)}) %collective-permute-start.1) | collective-permute-done | bytes 589856 | tf_op jit(solution)/shard_map/ppermute | solution.py:260
  126.2 3.2 %shard_map.108 = (f32[8,64,1024]{2,1,0:T(8,128)}, f32[8,64,128]{2,1,0:T(8,128)}) custom-call(bf16[256,1152]{1,0:T(8,128)(2,1)} %bitcast.9.mine, bf16[256,1152]{1,0:T(8,128)(2,1)S(1)} %collective-permute-done.1.theirs), custom_call_target="tpu_custom_call" | custom-call | flops 301989888 | bytes 3538944 | tf_op jit(solution)/shard_map/pallas_call | solution.py:46
  129.4 6.4 %reduce-scatter.2.cloned.1.call-done = bf16[64,1024]{1,0:T(8,128)(2,1)} async-done(((bf16[512,1024]{1,0:T(8,128)(2,1)}), bf16[64,1024]{1,0:T(8,128)(2,1)}) %reduce-scatter.2.cloned.1.call-update) | async-done | bytes 131088 | tf_op jit(solution)/shard_map/reduce_scatter | solution.py:248
  135.8 1.6 %add_convert_fusion = bf16[64,1024]{1,0:T(8,128)(2,1)} fusion(f32[64,1024]{1,0:T(8,128)S(1)} %get-tuple-element.22, bf16[64,1024]{1,0:T(8,128)(2,1)} %reduce-scatter.2.cloned.1.call-done), kind=kLoop, calls=%fused_computation | loop fusion | flops 196608 | bytes 524288 | tf_op jit(solution)/shard_map/convert_element_type | solution.py:266
  (23 shorter events, 4.1 us)
Async XLA Ops:
  8.6 19.6 %all-to-all-start = ((bf16[4,16,1024]{2,1,0:T(8,128)(2,1)}), bf16[4,16,1024]{2,1,0:T(8,128)(2,1)S(1)}, u32[]{:S(2)}, u32[]{:S(2)}) async-start(bf16[4,16,1024]{2,1,0:T(8,128)(2,1)} %broadcast_in_dim.3), calls=%async_computation | async-start | bytes 262144 | tf_op jit(solution)/shard_map/all_to_all | solution.py:217
  28.2 0.7 copy-start.9
  28.2 29.9 %copy-start = (bf16[512,1024]{1,0:T(8,128)(2,1)S(1)}, bf16[512,1024]{1,0:T(8,128)(2,1)}, u32[]{:S(2)}) copy-start(bf16[512,1024]{1,0:T(8,128)(2,1)} %tokens.3) | copy-start | bytes 3145732
  28.8 29.2 %all-to-all-start.1 = ((bf16[8,1024,128]{2,1,0:T(8,128)(2,1)}), bf16[8,1024,128]{2,1,0:T(8,128)(2,1)S(1)}, u32[]{:S(2)}, u32[]{:S(2)}) async-start(bf16[8,1024,128]{2,1,0:T(8,128)(2,1)} %shard_map.103), calls=%async_computation.2 | async-start | bytes 4194304 | tf_op jit(solution)/shard_map/all_to_all | solution.py:231
  33.1 30.1 %copy-start.7 = (s32[256,1]{0,1:T(1,128)S(1)}, s32[256,1]{0,1:T(1,128)}, u32[]{:S(2)}) copy-start(s32[256,1]{0,1:T(1,128)} %param.12) | copy-start | bytes 3076
  33.1 41.3 %all-gather.3.cloned.1.call-start = ((), (), s32[]{:S(2)}) async-start(), calls=%async_computation.6 | async-start | bytes 2228224 | tf_op jit(solution)/shard_map/all_gather | solution.py:230
  59.7 3.5 %collective-permute-start = (bf16[128,1152]{1,0:T(8,128)(2,1)S(1)}, bf16[128,1152]{1,0:T(8,128)(2,1)S(1)}, u32[]{:S(2)}, u32[]{:S(2)}) collective-permute-start(bf16[128,1152]{1,0:T(8,128)(2,1)S(1)} %get-tuple-element.16), channel_id=1, source_target_pairs={{0,8},{8,0},{1,9},{9,1},{2,10},{10,2},{3,11},{11,3},{4,12},{12,4},... | collective-permute-start | bytes 884744 | tf_op jit(solution)/shard_map/ppermute | solution.py:244
  64.2 0.8 copy-start.5
  65.0 27.8 %all-to-all-start.2 = ((bf16[32,8,1152]{2,1,0:T(8,128)(2,1)}), bf16[32,8,1152]{2,1,0:T(8,128)(2,1)}, u32[]{:S(2)}, u32[]{:S(2)}) async-start(bf16[32,8,1152]{2,1,0:T(8,128)(2,1)} %bitcast.15), calls=%async_computation.3 | async-start | bytes 1179648 | tf_op jit(solution)/shard_map/all_to_all | solution.py:246
  74.4 61.4 %reduce-scatter.2.cloned.1.call-start = ((), (), s32[]{:S(2)}) async-start(), calls=%async_computation.5 | async-start | bytes 1179648 | tf_op jit(solution)/shard_map/reduce_scatter | solution.py:248
  74.4 1.6 %copy-start.1 = (bf16[4,256,1024]{2,1,0:T(8,128)(2,1)S(1)}, bf16[4,256,1024]{2,1,0:T(8,128)(2,1)}, u32[]{:S(2)}) copy-start(bf16[4,256,1024]{2,1,0:T(8,128)(2,1)} %all-gather.3.cloned.1.call-done) | copy-start | bytes 6291460
  76.0 16.8 %copy-start.8 = (s32[256]{0:T(256)S(1)}, s32[256]{0:T(256)}, u32[]{:S(2)}) copy-start(s32[256]{0:T(256)} %live.1) | copy-start | bytes 3076
  77.3 1.0 copy-start.3
  78.3 25.1 %copy-start.4 = (bf16[8,1024,64]{1,2,0:T(8,128)(2,1)S(1)}, bf16[8,1024,64]{1,2,0:T(8,128)(2,1)}, u32[]{:S(2)}) copy-start(bf16[8,1024,64]{1,2,0:T(8,128)(2,1)} %param.9) | copy-start | bytes 3145732
  94.1 0.8 copy-start.6
  94.9 27.1 %all-to-all-start.3 = ((bf16[32,8,1152]{2,1,0:T(8,128)(2,1)}), bf16[32,8,1152]{2,1,0:T(8,128)(2,1)}, u32[]{:S(2)}, u32[]{:S(2)}) async-start(bf16[32,8,1152]{2,1,0:T(8,128)(2,1)} %bitcast.16), calls=%async_computation.4 | async-start | bytes 1179648 | tf_op jit(solution)/shard_map/all_to_all | solution.py:254
  103.4 1.6 %copy-start.2 = (bf16[4,256,1024]{2,1,0:T(8,128)(2,1)S(1)}, bf16[4,256,1024]{2,1,0:T(8,128)(2,1)}, u32[]{:S(2)}) copy-start(bf16[4,256,1024]{2,1,0:T(8,128)(2,1)} %all-gather.3.cloned.1.call-done) | copy-start | bytes 6291460
  122.1 4.1 %collective-permute-start.1 = (bf16[256,1152]{1,0:T(8,128)(2,1)}, bf16[256,1152]{1,0:T(8,128)(2,1)S(1)}, u32[]{:S(2)}, u32[]{:S(2)}) collective-permute-start(bf16[256,1152]{1,0:T(8,128)(2,1)} %bitcast.9.mine), channel_id=1, source_target_pairs={{0,8},{8,0},{1,9},{9,1},{2,10},{10,2},{3,11},{11,3},{4,12},{12,4},... | collective-permute-start | bytes 1769480 | tf_op jit(solution)/shard_map/ppermute | solution.py:260
Sparse Core Ops, SparseCore 0:
  36.7 37.3 all-gather.2
  78.4 57.2 reduce-scatter.1
